TPU v7x, 256 devices: a whole 4x4x8 slice. The times are simulated.
256 devices in a mesh: dp: 4 (over z_lo), ctx: 64 (over y, x, z_hi, core).
Axes of the slice: x: 4, y: 4, z: 8 (z_hi: 2, z_lo: 4; z = z_hi * 4 + z_lo), core: 2. Of those that a mesh axis runs over, the one named last changes fastest.
Arguments:
- queries: bfloat16 [4, 64, 128, 1024], P('dp', 'ctx'), may hold values from -256 to 256
- keys: bfloat16 [4, 64, 128, 1024], P('dp', 'ctx'), may hold values from -6 to 6
- values: bfloat16 [4, 64, 128, 1024], P('dp', 'ctx'), may hold values from -6 to 6
- d_out: bfloat16 [4, 64, 128, 1024], P('dp', 'ctx'), may hold values from -6 to 6
- out_weight: bfloat16 [1024, 1024], P('ctx'), may hold values from -0.1875 to 0.1875
- bar_lengths: int32 [4, 64], P('dp'), may hold values from 1 to 128, as said below
- summary_pos: int32 [4, 64], P('dp'), may hold values from 0 to 127, as said below
Outputs:
- d_queries: bfloat16 [4, 64, 128, 1024], P('dp', 'ctx')
- d_keys: bfloat16 [4, 64, 128, 1024], P('dp', 'ctx')
- d_values: bfloat16 [4, 64, 128, 1024], P('dp', 'ctx')
- d_weight: float32 [1024, 1024], P('ctx')
Inputs may be any that keep to these rules, and one draw needn't show every extreme that they name: `bar_lengths`: the first bar of each score is full (128) and the second holds one token. summary_pos of a bar is below that bar's length.
All inputs are finite; a program needn't handle non-finite values.
Results may differ from a plain program's by a relative error of at most 0.0062.
Values may be sent and summed in bfloat16 or wider, within the bound.
A program may use at most 64 MiB of HBM per device.

v0:
```python
import jax
import jax.numpy as jnp
import numpy as np
from jax import lax
from jax.sharding import PartitionSpec as P

HEADS = 16


structure_offsets = (1, 2, 4, 8, 12, 16, 24, 32)


def shifted(value, axis, steps):
    count = lax.axis_size(axis)
    leading, last = (max(0, -steps), min(count, count - steps))
    return lax.ppermute(value, axis, [(source, source + steps) for source in range(leading, last)])


def shortened(shard):

    def short(part):
        return part.astype(jnp.bfloat16) if part.dtype == jnp.float32 else part

    return jax.tree.map(short, shard)


def join_heads(stacked):
    moved = jnp.moveaxis(stacked, 0, -2)
    return moved.reshape(moved.shape[:-2] + (-1,))


def on_device(queries, keys, values, d_out, out_weight, bar_lengths, summary_pos):
    q_bars = queries[0]
    k_bars = keys[0]
    v_bars = values[0]
    g_bars = d_out[0]
    per_dev, bar, width = q_bars.shape
    head = width // HEADS
    scale = head ** (-0.5)
    ctx_size = lax.axis_size("ctx")
    first = lax.axis_index("ctx") * per_dev
    lengths = bar_lengths[0]
    spots = summary_pos[0]
    nbars = lengths.shape[0]
    rows = per_dev * bar
    flat_g = g_bars.reshape(rows, width)
    d_attn = lax.dot_general(
        flat_g,
        lax.all_gather(out_weight, "ctx", axis=0, tiled=True),
        (((1,), (1,)), ((), ())),
        preferred_element_type=jnp.float32,
    )
    d_attn = d_attn.astype(jnp.bfloat16).reshape(per_dev, bar, width)
    places = [
        [(-((j - o) // per_dev), (j - o) % per_dev) for o in structure_offsets]
        for j in range(per_dev)
    ]
    distances = sorted({place[0] for line in places for place in line if place[0] > 0})
    pool_k = {0: k_bars}
    pool_v = {0: v_bars}
    for distance in distances:
        if distance < ctx_size:
            far_k, far_v = shifted((k_bars, v_bars), "ctx", distance)
        else:
            far_k, far_v = (jnp.zeros_like(k_bars), jnp.zeros_like(v_bars))
        pool_k[distance] = far_k
        pool_v[distance] = far_v
    k_fine = jnp.stack(
        [jnp.stack([k_bars[j]] + [pool_k[d][s] for d, s in places[j]]) for j in range(per_dev)]
    )
    v_fine = jnp.stack(
        [jnp.stack([v_bars[j]] + [pool_v[d][s] for d, s in places[j]]) for j in range(per_dev)]
    )
    nlist = k_fine.shape[1]
    nfine = nlist * bar
    tpos = jnp.arange(bar, dtype=jnp.int32)
    local_ids = first + jnp.arange(per_dev, dtype=jnp.int32)
    own_len = lax.dynamic_slice_in_dim(lengths, first, per_dev)
    own_mask = (tpos[None, :, None] >= tpos[None, None, :]) & (
        tpos[None, None, :] < own_len[:, None, None]
    )
    rel = np.array([[j - o for o in structure_offsets] for j in range(per_dev)], np.int32)
    source = first + jnp.asarray(rel)
    source_len = jnp.where(source >= 0, lengths[jnp.clip(source, 0, nbars - 1)], 0)
    far_mask = (tpos[None, None, :] < source_len[:, :, None]).reshape(per_dev, 1, nfine - bar)
    far_mask = jnp.broadcast_to(far_mask, (per_dev, bar, nfine - bar))
    bar_ids = jnp.arange(nbars, dtype=jnp.int32)
    sum_mask = jnp.broadcast_to(
        (bar_ids[None, :] < local_ids[:, None])[:, None, :], (per_dev, bar, nbars)
    )
    mask = jnp.concatenate([own_mask, far_mask, sum_mask], axis=2)
    local_spots = lax.dynamic_slice_in_dim(spots, first, per_dev)
    pick = local_spots[:, None, None]
    own_sum_k = jnp.take_along_axis(k_bars, pick, axis=1)[:, 0]
    own_sum_v = jnp.take_along_axis(v_bars, pick, axis=1)[:, 0]
    sum_k, sum_v = (
        lax.all_gather(own_sum_k, "ctx", axis=0, tiled=True),
        lax.all_gather(own_sum_v, "ctx", axis=0, tiled=True),
    )

    def one_head(index):
        low = index * head

        def cut(block):
            return lax.dynamic_slice_in_dim(block, low, head, block.ndim - 1)

        q_head = cut(q_bars)
        g_head = cut(d_attn)
        k_all = cut(k_fine).reshape(per_dev, nfine, head)
        v_all = cut(v_fine).reshape(per_dev, nfine, head)
        k_sum = cut(sum_k)
        v_sum = cut(sum_v)
        s_fine = (
            jnp.einsum("bte,bse->bts", q_head, k_all, preferred_element_type=jnp.float32) * scale
        )
        s_sum = jnp.einsum("bte,ce->btc", q_head, k_sum, preferred_element_type=jnp.float32) * scale
        scores = jnp.where(mask, jnp.concatenate([s_fine, s_sum], axis=2), -jnp.inf)
        top = jnp.max(scores, axis=2, keepdims=True)
        expo = jnp.exp(scores - top)
        probs = expo / jnp.sum(expo, axis=2, keepdims=True)
        weights = probs.astype(jnp.bfloat16)
        p_fine = weights[:, :, :nfine]
        p_sum = weights[:, :, nfine:]
        attn = jnp.einsum("bts,bse->bte", p_fine, v_all, preferred_element_type=jnp.float32)
        attn = attn + jnp.einsum("btc,ce->bte", p_sum, v_sum, preferred_element_type=jnp.float32)
        delta = jnp.sum(g_head.astype(jnp.float32) * attn, axis=2, keepdims=True)
        dp_fine = jnp.einsum("bte,bse->bts", g_head, v_all, preferred_element_type=jnp.float32)
        dp_sum = jnp.einsum("bte,ce->btc", g_head, v_sum, preferred_element_type=jnp.float32)
        ds = (probs * (jnp.concatenate([dp_fine, dp_sum], axis=2) - delta)).astype(jnp.bfloat16)
        ds_fine = ds[:, :, :nfine]
        ds_sum = ds[:, :, nfine:]
        d_q = jnp.einsum("bts,bse->bte", ds_fine, k_all, preferred_element_type=jnp.float32)
        d_q = (
            d_q + jnp.einsum("btc,ce->bte", ds_sum, k_sum, preferred_element_type=jnp.float32)
        ) * scale
        dk_terms = (
            jnp.einsum("bts,bte->bse", ds_fine, q_head, preferred_element_type=jnp.float32) * scale
        )
        dv_terms = jnp.einsum("bts,bte->bse", p_fine, g_head, preferred_element_type=jnp.float32)
        dk_terms = dk_terms.reshape(per_dev, nlist, bar, head)
        dv_terms = dv_terms.reshape(per_dev, nlist, bar, head)
        dk_sum = (
            jnp.einsum("btc,bte->ce", ds_sum, q_head, preferred_element_type=jnp.float32) * scale
        )
        dv_sum = jnp.einsum("btc,bte->ce", p_sum, g_head, preferred_element_type=jnp.float32)
        local_k = [dk_terms[j, 0] for j in range(per_dev)]
        local_v = [dv_terms[j, 0] for j in range(per_dev)]
        far_k = {
            d: [jnp.zeros((bar, head), jnp.float32) for s in range(per_dev)] for d in distances
        }
        far_v = {
            d: [jnp.zeros((bar, head), jnp.float32) for s in range(per_dev)] for d in distances
        }
        for j in range(per_dev):
            for slot, place in enumerate(places[j]):
                distance, target = place
                if distance == 0:
                    local_k[target] = local_k[target] + dk_terms[j, 1 + slot]
                    local_v[target] = local_v[target] + dv_terms[j, 1 + slot]
                else:
                    far_k[distance][target] = far_k[distance][target] + dk_terms[j, 1 + slot]
                    far_v[distance][target] = far_v[distance][target] + dv_terms[j, 1 + slot]
        part_k = jnp.stack([jnp.stack(far_k[d]) for d in distances]).astype(jnp.bfloat16)
        part_v = jnp.stack([jnp.stack(far_v[d]) for d in distances]).astype(jnp.bfloat16)
        return (
            d_q.astype(jnp.bfloat16),
            jnp.stack(local_k),
            jnp.stack(local_v),
            part_k,
            part_v,
            dk_sum,
            dv_sum,
            attn.astype(jnp.bfloat16),
        )

    outputs = lax.map(one_head, jnp.arange(HEADS, dtype=jnp.int32))
    d_q = join_heads(outputs[0])
    total_k = join_heads(outputs[1])
    total_v = join_heads(outputs[2])
    part_k = join_heads(outputs[3])
    part_v = join_heads(outputs[4])
    dk_sum = join_heads(outputs[5])
    dv_sum = join_heads(outputs[6])
    attn_flat = join_heads(outputs[7]).reshape(rows, width)
    for index, distance in enumerate(distances):
        if distance < ctx_size:
            back_k, back_v = shifted(
                (shortened(part_k[index]), shortened(part_v[index])), "ctx", -distance
            )
            total_k = total_k + back_k.astype(jnp.float32)
            total_v = total_v + back_v.astype(jnp.float32)
    share_k, share_v = (
        lax.psum_scatter(dk_sum, "ctx", scatter_dimension=0, tiled=True),
        lax.psum_scatter(dv_sum, "ctx", scatter_dimension=0, tiled=True),
    )
    onehot = (tpos[None, :] == local_spots[:, None]).astype(jnp.float32)
    total_k = total_k + onehot[:, :, None] * share_k[:, None, :]
    total_v = total_v + onehot[:, :, None] * share_v[:, None, :]
    whole = lax.dot_general(
        attn_flat, flat_g, (((0,), (0,)), ((), ())), preferred_element_type=jnp.float32
    )
    whole = lax.psum(whole, "dp")
    d_weight = lax.psum_scatter(whole, "ctx", scatter_dimension=0, tiled=True)
    return (
        d_q[None],
        total_k.astype(jnp.bfloat16)[None],
        total_v.astype(jnp.bfloat16)[None],
        d_weight,
    )


def solution(mesh):
    in_specs = (
        P("dp", "ctx", None, None),
        P("dp", "ctx", None, None),
        P("dp", "ctx", None, None),
        P("dp", "ctx", None, None),
        P("ctx", None),
        P("dp", None),
        P("dp", None),
    )
    out_specs = (
        P("dp", "ctx", None, None),
        P("dp", "ctx", None, None),
        P("dp", "ctx", None, None),
        P("ctx", None),
    )
    return jax.shard_map(
        on_device, mesh=mesh, in_specs=in_specs, out_specs=out_specs, check_vma=False
    )
```

profile of v0, /device:TPU:2, one launch (start us, length us, event | category | flops | bytes accessed | tf_op | source)
XLA Modules:
  0.0 1872.2 jit_solution(13917519009203151219)
XLA Ops:
  7.2 2.1 collective-permute-start
  9.3 9.1 collective-permute-start.1
  18.4 3.4 collective-permute-start.2
  21.8 4.8 collective-permute-start.3
  26.6 4.0 collective-permute-start.4
  41.7 105.7 %all-gather.1 = bf16[64,1,1024]{2,1,0:T(2,128)(2,1)S(1)} all-gather(bf16[1,1,1024]{2,1,0:T(2,128)(2,1)S(1)} %broadcast_select_fusion), channel_id=3, replica_groups=mesh['dp'=4,'ctx'=64] {'ctx'}, dimensions={0}, use_global_device_ids=true | all-gather | bytes 133120 | tf_op jit(solution)/shard_map/all_gather | solution.py:98
  147.4 115.0 %all-gather = bf16[64,1,1024]{2,1,0:T(2,128)(2,1)S(1)} all-gather(bf16[1,1,1024]{2,1,0:T(2,128)(2,1)S(1)} %broadcast_select_fusion.1), channel_id=2, replica_groups=mesh['dp'=4,'ctx'=64] {'ctx'}, dimensions={0}, use_global_device_ids=true | all-gather | bytes 133120 | tf_op jit(solution)/shard_map/all_gather | solution.py:97
  269.0 4.9 collective-permute-start.7
  274.9 1.9 collective-permute-start.8
  277.9 4.6 collective-permute-start.9
  283.5 1.9 collective-permute-start.10
  285.4 2.5 collective-permute-start.11
  288.0 2.8 collective-permute-start.12
  290.8 27.1 %collective-permute-start.13 = (bf16[1,128,1024]{2,1,0:T(8,128)(2,1)S(1)}, bf16[1,128,1024]{2,1,0:T(8,128)(2,1)S(1)}, u32[]{:S(2)}, u32[]{:S(2)}) collective-permute-start(bf16[1,128,1024]{2,1,0:T(8,128)(2,1)S(1)} %bitcast.351), channel_id=1, source_target_pairs={{0,16},{1,17},{2,18},{3,19},{4,20},{5,21},{6,22},{7,23},{8,24},{9,... | collective-permute-start | bytes 786440 | tf_op jit(solution)/shard_map/ppermute | solution.py:16
  320.7 3.9 collective-permute-done.13
  324.7 4.2 collective-permute-done.15
  330.4 3.1 fusion.50
  335.2 268.7 %while.25 = (s32[]{:T(128)}, bf16[16,1,128,64]{2,3,1,0:T(8,128)(2,1)}, f32[16,1,128,64]{2,1,3,0:T(1,128)S(1)}, f32[16,1,128,64]{2,3,1,0:T(8,128)}, bf16[16,8,1,1...) while((s32[]{:T(128)}, ...), condition=%wide.region_4.6_spmd, body=%wide.region_0.5_spmd.sunk | while | flops 123096704 | bytes 13658911 | solution.py:176
  608.6 2.7 fusion.51
  611.3 2.6 fusion.61
  614.0 2.0 collective-permute-start.24
  616.0 11.3 collective-permute-start.25
  627.3 1.9 collective-permute-start.26
  634.5 2.8 collective-permute-done.25
  641.4 4.3 collective-permute-start.16
  645.7 3.1 collective-permute-start.17
  648.9 4.6 collective-permute-done.29
  653.5 1.9 collective-permute-start.18
  656.7 1.8 copy.260
  658.5 735.4 %all-reduce.8.cloned.1.call-done = (f32[64,1024]{1,0:T(8,128)}, f32[64,1024]{1,0:T(8,128)}) async-done(((f32[64,1024]{1,0:T(8,128)}, f32[64,1024]{1,0:T(8,128)}), (f32[64,1024]{1,0:T(8,128)}, f32[64,1024]{1,0:T(8,128)})) %all-reduce.8.cloned.1.call-update) | async-done | bytes 524304
  1405.0 400.8 %reduce-scatter.2.cloned.1.call-done = f32[16,1024]{1,0:T(8,128)} async-done(((f32[1024,1024]{1,0:T(8,128)}), f32[16,1024]{1,0:T(8,128)}) %reduce-scatter.2.cloned.1.call-update) | async-done | bytes 65552 | tf_op jit(solution)/shard_map/reduce_scatter | solution.py:203
  1809.0 55.2 %all-reduce.6.cloned.1.call-done = f32[16,1024]{1,0:T(8,128)} async-done(((f32[16,1024]{1,0:T(8,128)}), f32[16,1024]{1,0:T(8,128)}) %all-reduce.6.cloned.1.call-update) | async-done | bytes 65552 | tf_op jit(solution)/shard_map/psum | solution.py:202
  (852 shorter events, 310.0 us)
Async XLA Ops:
  7.2 321.9 %all-gather.4.cloned.1.call-start = ((), (), s32[]{:S(2)}) async-start(), calls=%async_computation.1 | async-start | bytes 2129920 | tf_op jit(solution)/shard_map/all_gather | solution.py:49
  7.2 257.2 %collective-permute-start = (bf16[1,128,1024]{2,1,0:T(8,128)(2,1)}, bf16[1,128,1024]{2,1,0:T(8,128)(2,1)}, u32[]{:S(2)}, u32[]{:S(2)}) collective-permute-start(bf16[1,128,1024]{2,1,0:T(8,128)(2,1)} %bitcast.336), channel_id=1, source_target_pairs={{0,1},{1,2},{2,3},{3,4},{4,5},{5,6},{6,7},{7,8},{8,9},{9,10},{10,1... | collective-permute-start | bytes 786440 | tf_op jit(solution)/shard_map/ppermute | solution.py:16
  9.3 257.4 %collective-permute-start.1 = (bf16[1,128,1024]{2,1,0:T(8,128)(2,1)}, bf16[1,128,1024]{2,1,0:T(8,128)(2,1)}, u32[]{:S(2)}, u32[]{:S(2)}) collective-permute-start(bf16[1,128,1024]{2,1,0:T(8,128)(2,1)} %bitcast.337), channel_id=1, source_target_pairs={{0,2},{1,3},{2,4},{3,5},{4,6},{5,7},{6,8},{7,9},{8,10},{9,11},{10,... | collective-permute-start | bytes 786440 | tf_op jit(solution)/shard_map/ppermute | solution.py:16
  18.4 250.6 %collective-permute-start.2 = (bf16[1,128,1024]{2,1,0:T(8,128)(2,1)}, bf16[1,128,1024]{2,1,0:T(8,128)(2,1)}, u32[]{:S(2)}, u32[]{:S(2)}) collective-permute-start(bf16[1,128,1024]{2,1,0:T(8,128)(2,1)} %bitcast.338), channel_id=1, source_target_pairs={{0,4},{1,5},{2,6},{3,7},{4,8},{5,9},{6,10},{7,11},{8,12},{9,13},{1... | collective-permute-start | bytes 786440 | tf_op jit(solution)/shard_map/ppermute | solution.py:16
  21.8 253.1 %collective-permute-start.3 = (bf16[1,128,1024]{2,1,0:T(8,128)(2,1)}, bf16[1,128,1024]{2,1,0:T(8,128)(2,1)}, u32[]{:S(2)}, u32[]{:S(2)}) collective-permute-start(bf16[1,128,1024]{2,1,0:T(8,128)(2,1)} %bitcast.339), channel_id=1, source_target_pairs={{0,8},{1,9},{2,10},{3,11},{4,12},{5,13},{6,14},{7,15},{8,16},{9,17... | collective-permute-start | bytes 786440 | tf_op jit(solution)/shard_map/ppermute | solution.py:16
  26.6 251.3 %collective-permute-start.4 = (bf16[1,128,1024]{2,1,0:T(8,128)(2,1)}, bf16[1,128,1024]{2,1,0:T(8,128)(2,1)}, u32[]{:S(2)}, u32[]{:S(2)}) collective-permute-start(bf16[1,128,1024]{2,1,0:T(8,128)(2,1)} %bitcast.340), channel_id=1, source_target_pairs={{0,12},{1,13},{2,14},{3,15},{4,16},{5,17},{6,18},{7,19},{8,20},{9,... | collective-permute-start | bytes 786440 | tf_op jit(solution)/shard_map/ppermute | solution.py:16
  30.6 1363.3 %all-reduce.8.cloned.1.call-start = ((), (), s32[]{:S(2)}) async-start(), calls=%async_computation.4 | async-start | bytes 1048576
  264.4 19.0 %collective-permute-start.5 = (bf16[1,128,1024]{2,1,0:T(8,128)(2,1)}, bf16[1,128,1024]{2,1,0:T(8,128)(2,1)S(1)}, u32[]{:S(2)}, u32[]{:S(2)}) collective-permute-start(bf16[1,128,1024]{2,1,0:T(8,128)(2,1)} %bitcast.342), channel_id=1, source_target_pairs={{0,16},{1,17},{2,18},{3,19},{4,20},{5,21},{6,22},{7,23},{8,24},{9,... | collective-permute-start | bytes 786440 | tf_op jit(solution)/shard_map/ppermute | solution.py:16
  266.7 18.7 collective-permute-start.6
  269.0 18.9 %collective-permute-start.7 = (bf16[1,128,1024]{2,1,0:T(8,128)(2,1)S(1)}, bf16[1,128,1024]{2,1,0:T(8,128)(2,1)S(1)}, u32[]{:S(2)}, u32[]{:S(2)}) collective-permute-start(bf16[1,128,1024]{2,1,0:T(8,128)(2,1)S(1)} %bitcast.344), channel_id=1, source_target_pairs={{0,32},{1,33},{2,34},{3,35},{4,36},{5,37},{6,38},{7,39},{8,40},{9,... | collective-permute-start | bytes 786440 | tf_op jit(solution)/shard_map/ppermute | solution.py:16
  274.9 15.8 collective-permute-start.8
  277.9 40.0 %collective-permute-start.9 = (bf16[1,128,1024]{2,1,0:T(8,128)(2,1)S(1)}, bf16[1,128,1024]{2,1,0:T(8,128)(2,1)S(1)}, u32[]{:S(2)}, u32[]{:S(2)}) collective-permute-start(bf16[1,128,1024]{2,1,0:T(8,128)(2,1)S(1)} %bitcast.347), channel_id=1, source_target_pairs={{0,2},{1,3},{2,4},{3,5},{4,6},{5,7},{6,8},{7,9},{8,10},{9,11},{10,... | collective-permute-start | bytes 786440 | tf_op jit(solution)/shard_map/ppermute | solution.py:16
  283.5 35.8 %collective-permute-start.10 = (bf16[1,128,1024]{2,1,0:T(8,128)(2,1)S(1)}, bf16[1,128,1024]{2,1,0:T(8,128)(2,1)S(1)}, u32[]{:S(2)}, u32[]{:S(2)}) collective-permute-start(bf16[1,128,1024]{2,1,0:T(8,128)(2,1)S(1)} %bitcast.348), channel_id=1, source_target_pairs={{0,4},{1,5},{2,6},{3,7},{4,8},{5,9},{6,10},{7,11},{8,12},{9,13},{1... | collective-permute-start | bytes 786440 | tf_op jit(solution)/shard_map/ppermute | solution.py:16
  285.4 35.2 %collective-permute-start.11 = (bf16[1,128,1024]{2,1,0:T(8,128)(2,1)S(1)}, bf16[1,128,1024]{2,1,0:T(8,128)(2,1)S(1)}, u32[]{:S(2)}, u32[]{:S(2)}) collective-permute-start(bf16[1,128,1024]{2,1,0:T(8,128)(2,1)S(1)} %bitcast.349), channel_id=1, source_target_pairs={{0,8},{1,9},{2,10},{3,11},{4,12},{5,13},{6,14},{7,15},{8,16},{9,17... | collective-permute-start | bytes 786440 | tf_op jit(solution)/shard_map/ppermute | solution.py:16
  288.0 32.7 %collective-permute-start.12 = (bf16[1,128,1024]{2,1,0:T(8,128)(2,1)S(1)}, bf16[1,128,1024]{2,1,0:T(8,128)(2,1)S(1)}, u32[]{:S(2)}, u32[]{:S(2)}) collective-permute-start(bf16[1,128,1024]{2,1,0:T(8,128)(2,1)S(1)} %bitcast.350), channel_id=1, source_target_pairs={{0,12},{1,13},{2,14},{3,15},{4,16},{5,17},{6,18},{7,19},{8,20},{9,... | collective-permute-start | bytes 786440 | tf_op jit(solution)/shard_map/ppermute | solution.py:16
  290.8 33.8 %collective-permute-start.13 = (bf16[1,128,1024]{2,1,0:T(8,128)(2,1)S(1)}, bf16[1,128,1024]{2,1,0:T(8,128)(2,1)S(1)}, u32[]{:S(2)}, u32[]{:S(2)}) collective-permute-start(bf16[1,128,1024]{2,1,0:T(8,128)(2,1)S(1)} %bitcast.351), channel_id=1, source_target_pairs={{0,16},{1,17},{2,18},{3,19},{4,20},{5,21},{6,22},{7,23},{8,24},{9,... | collective-permute-start | bytes 786440 | tf_op jit(solution)/shard_map/ppermute | solution.py:16
  608.5 1197.2 %reduce-scatter.2.cloned.1.call-start = ((), (), s32[]{:S(2)}) async-start(), calls=%async_computation.2 | async-start | bytes 4259840 | tf_op jit(solution)/shard_map/reduce_scatter | solution.py:203
  611.3 1252.9 %all-reduce.6.cloned.1.call-start = ((), (), s32[]{:S(2)}) async-start(), calls=%async_computation.3 | async-start | bytes 131072 | tf_op jit(solution)/shard_map/psum | solution.py:202
  614.0 17.9 collective-permute-start.24
  616.0 21.4 %collective-permute-start.25 = (bf16[1,128,1024]{1,2,0:T(8,128)(2,1)S(1)}, bf16[1,128,1024]{1,2,0:T(8,128)(2,1)}, u32[]{:S(2)}, u32[]{:S(2)}) collective-permute-start(bf16[1,128,1024]{1,2,0:T(8,128)(2,1)S(1)} %bitcast.364), channel_id=1, source_target_pairs={{2,0},{3,1},{4,2},{5,3},{6,4},{7,5},{8,6},{9,7},{10,8},{11,9},{12,... | collective-permute-start | bytes 786440 | tf_op jit(solution)/shard_map/ppermute | solution.py:16
  630.5 15.2 collective-permute-start.28
  631.9 21.6 %collective-permute-start.29 = (bf16[1,128,1024]{1,2,0:T(8,128)(2,1)S(1)}, bf16[1,128,1024]{1,2,0:T(8,128)(2,1)}, u32[]{:S(2)}, u32[]{:S(2)}) collective-permute-start(bf16[1,128,1024]{1,2,0:T(8,128)(2,1)S(1)} %bitcast.360), channel_id=1, source_target_pairs={{16,0},{17,1},{18,2},{19,3},{20,4},{21,5},{22,6},{23,7},{24,8},{25... | collective-permute-start | bytes 786440 | tf_op jit(solution)/shard_map/ppermute | solution.py:16
  637.4 759.4 %collective-permute-start.30 = (bf16[1,128,1024]{1,2,0:T(8,128)(2,1)}, bf16[1,128,1024]{1,2,0:T(8,128)(2,1)S(1)}, u32[]{:S(2)}, u32[]{:S(2)}) collective-permute-start(bf16[1,128,1024]{1,2,0:T(8,128)(2,1)} %bitcast.79), channel_id=1, source_target_pairs={{24,0},{25,1},{26,2},{27,3},{28,4},{29,5},{30,6},{31,7},{32,8},{33... | collective-permute-start | bytes 786440 | tf_op jit(solution)/shard_map/ppermute | solution.py:16
  640.1 758.0 %collective-permute-start.31 = (bf16[1,128,1024]{1,2,0:T(8,128)(2,1)}, bf16[1,128,1024]{1,2,0:T(8,128)(2,1)S(1)}, u32[]{:S(2)}, u32[]{:S(2)}) collective-permute-start(bf16[1,128,1024]{1,2,0:T(8,128)(2,1)} %bitcast.80), channel_id=1, source_target_pairs={{32,0},{33,1},{34,2},{35,3},{36,4},{37,5},{38,6},{39,7},{40,8},{41... | collective-permute-start | bytes 786440 | tf_op jit(solution)/shard_map/ppermute | solution.py:16
  641.4 758.0 %collective-permute-start.16 = (bf16[1,128,1024]{1,2,0:T(8,128)(2,1)}, bf16[1,128,1024]{1,2,0:T(8,128)(2,1)S(1)}, u32[]{:S(2)}, u32[]{:S(2)}) collective-permute-start(bf16[1,128,1024]{1,2,0:T(8,128)(2,1)} %bitcast.57), channel_id=1, source_target_pairs={{1,0},{2,1},{3,2},{4,3},{5,4},{6,5},{7,6},{8,7},{9,8},{10,9},{11,1... | collective-permute-start | bytes 786440 | tf_op jit(solution)/shard_map/ppermute | solution.py:16
  645.7 754.9 %collective-permute-start.17 = (bf16[1,128,1024]{1,2,0:T(8,128)(2,1)}, bf16[1,128,1024]{1,2,0:T(8,128)(2,1)S(1)}, u32[]{:S(2)}, u32[]{:S(2)}) collective-permute-start(bf16[1,128,1024]{1,2,0:T(8,128)(2,1)} %bitcast.58), channel_id=1, source_target_pairs={{2,0},{3,1},{4,2},{5,3},{6,4},{7,5},{8,6},{9,7},{10,8},{11,9},{12,... | collective-permute-start | bytes 786440 | tf_op jit(solution)/shard_map/ppermute | solution.py:16
  653.5 748.5 %collective-permute-start.18 = (bf16[1,128,1024]{1,2,0:T(8,128)(2,1)}, bf16[1,128,1024]{1,2,0:T(8,128)(2,1)S(1)}, u32[]{:S(2)}, u32[]{:S(2)}) collective-permute-start(bf16[1,128,1024]{1,2,0:T(8,128)(2,1)} %bitcast.59), channel_id=1, source_target_pairs={{4,0},{5,1},{6,2},{7,3},{8,4},{9,5},{10,6},{11,7},{12,8},{13,9},{1... | collective-permute-start | bytes 786440 | tf_op jit(solution)/shard_map/ppermute | solution.py:16
  1396.7 409.0 %collective-permute-start.19 = (bf16[1,128,1024]{1,2,0:T(8,128)(2,1)}, bf16[1,128,1024]{1,2,0:T(8,128)(2,1)S(1)}, u32[]{:S(2)}, u32[]{:S(2)}) collective-permute-start(bf16[1,128,1024]{1,2,0:T(8,128)(2,1)} %bitcast.359), channel_id=1, source_target_pairs={{8,0},{9,1},{10,2},{11,3},{12,4},{13,5},{14,6},{15,7},{16,8},{17,9... | collective-permute-start | bytes 786440 | tf_op jit(solution)/shard_map/ppermute | solution.py:16
  1398.1 407.7 %collective-permute-start.20 = (bf16[1,128,1024]{1,2,0:T(8,128)(2,1)}, bf16[1,128,1024]{1,2,0:T(8,128)(2,1)S(1)}, u32[]{:S(2)}, u32[]{:S(2)}) collective-permute-start(bf16[1,128,1024]{1,2,0:T(8,128)(2,1)} %bitcast.358), channel_id=1, source_target_pairs={{12,0},{13,1},{14,2},{15,3},{16,4},{17,5},{18,6},{19,7},{20,8},{21... | collective-permute-start | bytes 786440 | tf_op jit(solution)/shard_map/ppermute | solution.py:16
  1399.4 406.4 %collective-permute-start.21 = (bf16[1,128,1024]{1,2,0:T(8,128)(2,1)}, bf16[1,128,1024]{1,2,0:T(8,128)(2,1)}, u32[]{:S(2)}, u32[]{:S(2)}) collective-permute-start(bf16[1,128,1024]{1,2,0:T(8,128)(2,1)} %bitcast.357), channel_id=1, source_target_pairs={{16,0},{17,1},{18,2},{19,3},{20,4},{21,5},{22,6},{23,7},{24,8},{25... | collective-permute-start | bytes 786440 | tf_op jit(solution)/shard_map/ppermute | solution.py:16
  1400.7 405.1 %collective-permute-start.22 = (bf16[1,128,1024]{1,2,0:T(8,128)(2,1)}, bf16[1,128,1024]{1,2,0:T(8,128)(2,1)}, u32[]{:S(2)}, u32[]{:S(2)}) collective-permute-start(bf16[1,128,1024]{1,2,0:T(8,128)(2,1)} %bitcast.356), channel_id=1, source_target_pairs={{24,0},{25,1},{26,2},{27,3},{28,4},{29,5},{30,6},{31,7},{32,8},{33... | collective-permute-start | bytes 786440 | tf_op jit(solution)/shard_map/ppermute | solution.py:16
  1402.0 403.8 %collective-permute-start.23 = (bf16[1,128,1024]{1,2,0:T(8,128)(2,1)}, bf16[1,128,1024]{1,2,0:T(8,128)(2,1)}, u32[]{:S(2)}, u32[]{:S(2)}) collective-permute-start(bf16[1,128,1024]{1,2,0:T(8,128)(2,1)} %bitcast.355), channel_id=1, source_target_pairs={{32,0},{33,1},{34,2},{35,3},{36,4},{37,5},{38,6},{39,7},{40,8},{41... | collective-permute-start | bytes 786440 | tf_op jit(solution)/shard_map/ppermute | solution.py:16
  (15 other events, 1260.4 us)
Sparse Core Ops, SparseCore 0:
  30.8 80.0 all-gather.3
  608.6 785.2 all-reduce.7
  1396.6 409.1 reduce-scatter.1
  1808.2 55.9 all-reduce.5
where the time goes:
time: 1880 us; the launch traced here: 1870 us
  waiting for transfers between devices  1210 us (64%)
  blocking collectives  221 us (12%)
  matrix products  143 us (8%)
  local copies, waits for them, and re-layouts  134 us (7%)
  starting transfers between devices  112 us (6%)
  other arithmetic  23.5 us (1%)
    unnamed x5, waiting for transfers between devices  735 us
    reduce_scatter x1, waiting for transfers between devices, on_device(): d_weight = lax.psum_scatter(whole, 'ctx', scatter_dimension=0, tiled=True)  401 us
    all_gather x1, blocking collectives, on_device(): lax.all_gather(own_sum_k, 'ctx', axis=0, tiled=True)  115 us
    ppermute x32, starting transfers between devices, shifted(): lax.ppermute(value, axis, [(source, source + steps) for source in range(l...  112 us
    all_gather x1, blocking collectives, on_device(): lax.all_gather(own_sum_v, 'ctx', axis=0, tiled=True)  106 us
    psum x1, waiting for transfers between devices, on_device(): whole = lax.psum(whole, 'dp')  55.2 us
  transfers between devices with their start and end apart: 36, of which 9 were waited for; matrix products, arithmetic and copies ran while one was open for 2% of the time, Pallas kernels for 0%

commit v1 on v0

v1 whole, which is shorter than its diff:
```python
import jax
import jax.numpy as jnp
from jax import lax
from jax.experimental import pallas as pl
from jax.experimental.pallas import tpu as pltpu
from jax.sharding import PartitionSpec as P

N = 16
BAR = 128
HEAD = 64
WIDTH = 1024
PAD = 8
NKEYS = 1280
OWN_STEPS = (1, 2, 3, 4, 6, 8)
LOW = -1e30
MESH = pl.DeviceIdType.MESH
BF = jnp.bfloat16
F32 = jnp.float32


def remote(src, dst, send, recv, device):
    return pltpu.make_async_remote_copy(
        src_ref=src, dst_ref=dst, send_sem=send, recv_sem=recv, device_id=device, device_id_type=MESH
    )


def loop(low, high, body):
    def step(i, carry):
        body(i)
        return carry

    lax.fori_loop(low, high, step, 0)


def dot_nt(a, b):
    return lax.dot_general(a, b, (((1,), (1,)), ((), ())), preferred_element_type=F32)


def dot(a, b):
    return jnp.dot(a, b, preferred_element_type=F32)


def kernel(
    q_ref, k_ref, v_ref, do_ref, w_ref, len_ref, spot_ref,
    dq_ref, dk_ref, dv_ref, dw_ref,
    kvs, kvo, p1, p2, kvot, p1t, p2t, qgs, qgr, w4, do2, sumf, sumkv, sumt,
    b_ref, s_ref, x_ref, cat, catt, acc, accsum, d1s, d1r, d2s, d2r, d2f, sgr,
    fks, fkr, dqs, dqr, ats, atr, dws, dwr, wsum, zs, zr,
    kv_s, kv_r, p1_s, p1_r, p2_s, p2_r, wa_s, wa_r, wb_s, wb_r, wc_s, wc_r, do_s, do_r,
    qg_s, qg_r, sm_s, sm_r, d1_s, d1_rs, d2_s, d2_rs, sg_s, sg_rs, fk_s, fk_rs,
    dq_s, dq_rs, at_s, at_rs, dw_s, dw_rs, z_s, z_rs,
):
    dp = lax.axis_index("dp")
    ctx = lax.axis_index("ctx")
    i0 = lax.div(ctx, 4)
    r = lax.rem(ctx, 4)
    zh = lax.div(r, 2)
    core = lax.rem(r, 2)
    z = zh * 4 + dp
    odd = core == 1
    even = core == 0
    me = (dp, ctx)
    sib = (dp, 4 * i0 + 2 * zh + (1 - core))
    far = (dp, 4 * i0 + 2 * (1 - zh) + core)
    diag = (dp, 4 * i0 + 2 * (1 - zh) + (1 - core))

    def peer(j):
        return (dp, 4 * j + r)

    def near(j, c):
        return (dp, 4 * j + 2 * zh + c)

    def zpeer(t):
        return (lax.rem(t, 4), 4 * i0 + 2 * lax.div(t, 4) + core)

    def rot(d):
        return lax.rem(i0 + d, N)

    barrier = pltpu.get_barrier_semaphore()

    def greet(device):
        pl.semaphore_signal(barrier, inc=1, device_id=device, device_id_type=MESH)

    loop(0, N, lambda d: greet(near(rot(d), 1 - core)))
    loop(1, N, lambda d: greet(peer(rot(d))))
    loop(1, 8, lambda d: greet(zpeer(lax.rem(z + d, 8))))
    greet(diag)

    for p in range(N // 2):
        cols = slice(128 * p, 128 * p + 128)
        kk = k_ref[:, cols]
        vv = v_ref[:, cols]
        kvs[2 * p] = jnp.concatenate([kk[:, :HEAD], vv[:, :HEAD]], axis=1)
        kvs[2 * p + 1] = jnp.concatenate([kk[:, HEAD:], vv[:, HEAD:]], axis=1)
    zero = jnp.zeros((BAR, BAR), BF)
    for n in range(PAD):
        kvo[n] = zero
        kvot[n] = zero
    p1[0] = zero
    p1t[0] = zero
    p2[0] = zero
    p2t[0] = zero
    cat[pl.ds(1152, 128), :] = zero
    catt[:, pl.ds(1152, 128)] = zero
    x_ref[pl.ds(1152, 128), :] = jnp.zeros((128, 256), BF)
    acc[...] = jnp.zeros(acc.shape, F32)
    accsum[...] = jnp.zeros(accsum.shape, F32)
    kvo[PAD + i0] = kvs[i0]
    w4[i0, zh, core] = w_ref[...]
    do2[core] = do_ref[...]

    pl.semaphore_wait(barrier, 39)

    wa = remote(w4.at[i0, zh, core], w4.at[i0, zh, core], wa_s.at[0], wa_r.at[0], far)
    wa.start()

    def send_kv(d):
        j = rot(d)
        remote(kvs.at[j], kvo.at[PAD + i0], kv_s.at[j], kv_r.at[i0], peer(j)).start()

    loop(1, N, send_kv)
    do_copy = remote(do2.at[core], do2.at[core], do_s.at[0], do_r.at[0], sib)
    do_copy.start()
    remote(w4.at[i0, 1 - zh, core], w4.at[i0, 1 - zh, core], wa_s.at[0], wa_r.at[0], far).wait_recv()

    def send_w(d):
        j = rot(d)
        remote(w4.at[i0, :, core], w4.at[i0, :, core], wb_s.at[j], wb_r.at[i0], peer(j)).start()

    loop(1, N, send_w)

    row = lax.broadcasted_iota(jnp.int32, (BAR, BAR), 0)
    col = lax.broadcasted_iota(jnp.int32, (BAR, BAR), 1)

    def pass_on(j):
        @pl.when(j != i0)
        def _():
            remote(kvs.at[j], kvo.at[PAD + j], kv_s.at[j], kv_r.at[j], peer(j)).wait_recv()

        remote(kvo.at[PAD + j], p2.at[1 + j], p2_s.at[j], p2_r.at[j], far).start()

        @pl.when(even)
        def _():
            remote(kvo.at[PAD + j], p1.at[1 + j], p1_s.at[j], p1_r.at[j], sib).start()

        block = kvo[PAD + j]
        kvot[PAD + j] = block.T
        spot = spot_ref[0, 4 * j + r]
        picked = jnp.where(row == spot, block.astype(F32), 0.0)
        sumf[pl.ds(j, 1), :] = jnp.sum(picked, axis=0, keepdims=True)

    loop(0, N, pass_on)
    sumkv[r] = sumf[...].astype(BF)
    r_sib = 2 * zh + (1 - core)
    r_far = 2 * (1 - zh) + core
    r_diag = 2 * (1 - zh) + (1 - core)
    others = ((sib, r_sib), (far, r_far), (diag, r_diag))
    for device, rr in others:
        remote(sumkv.at[r], sumkv.at[r], sm_s.at[rr], sm_r.at[r], device).start()

    def pass_w(d):
        j = rot(d)

        @pl.when(d > 0)
        def _():
            remote(w4.at[j, :, core], w4.at[j, :, core], wb_s.at[j], wb_r.at[j], peer(j)).wait_recv()

        remote(w4.at[j, :, core], w4.at[j, :, core], wc_s.at[j], wc_r.at[j], sib).start()

    loop(0, N, pass_w)

    for c in range(4):
        for j in range(4 * c, 4 * c + 4):
            remote(w4.at[j, :, 1 - core], w4.at[j, :, 1 - core], wc_s.at[j], wc_r.at[j], sib).wait_recv()
        rows = w4[4 * c : 4 * c + 4].reshape(256, WIDTH)
        g = dot_nt(do_ref[...], rows).astype(BF)
        qq = (q_ref[:, 256 * c : 256 * c + 256].astype(F32) * 0.125).astype(BF)
        for h in range(4):
            cols = slice(HEAD * h, HEAD * h + HEAD)
            qgs[4 * c + h] = jnp.concatenate([qq[:, cols], g[:, cols]], axis=1)
        for h in range(4 * c, 4 * c + 4):
            @pl.when(i0 != h)
            def _():
                remote(qgs.at[h], qgr.at[i0], qg_s.at[h], qg_r.at[i0], peer(h)).start()

    qgr[i0] = qgs[i0]

    for device, rr in others:
        remote(sumkv.at[rr], sumkv.at[rr], sm_s.at[rr], sm_r.at[rr], device).wait_recv()
    cat[pl.ds(1152, 64), :] = sumkv[...].reshape(64, BAR)
    catt[:, pl.ds(1152, 128)] = cat[pl.ds(1152, 128), :].T

    lag1 = jnp.where(r < 1, 1, 0)
    lag2 = jnp.where(r < 2, 1, 0)
    srow = lax.broadcasted_iota(jnp.int32, (64, BAR), 0)
    sbar = 4 * lax.rem(srow, 16) + lax.div(srow, 16)
    left = col < HEAD

    def join(i):
        @pl.when(odd)
        def _():
            remote(d1s.at[i], d1r.at[i], d1_s.at[i], d1_rs.at[i], sib).wait_recv()
            d2s[i] = (d2f[lax.rem(i, 2)] + d1r[i].astype(F32)).astype(BF)
            remote(d2s.at[i], d2r.at[i], d2_s.at[i], d2_rs.at[i], far).start()

    def one_bar(i):
        bar = 4 * i + r

        @pl.when(i != i0)
        def _():
            remote(qgs.at[i], qgr.at[i], qg_s.at[i], qg_r.at[i], peer(i)).wait_recv()

        remote(kvo.at[PAD + i], p2.at[1 + i], p2_s.at[i], p2_r.at[i], far).wait_recv()

        @pl.when(odd)
        def _():
            remote(p2.at[1 + i], p1.at[1 + i], p1_s.at[i], p1_r.at[i], sib).start()

        remote(kvo.at[PAD + i], p1.at[1 + i], p1_s.at[i], p1_r.at[i], sib).wait_recv()
        p1t[1 + i] = p1[1 + i].T
        p2t[1 + i] = p2[1 + i].T

        blocks = [(kvo, kvot, PAD + i, 0), (p1, p1t, 1 + i - lag1, 1), (p2, p2t, 1 + i - lag2, 2)]
        blocks += [(kvo, kvot, PAD + i - m, 4 * m) for m in OWN_STEPS]
        lens = []
        for n, (src, srct, at, offset) in enumerate(blocks):
            cat[pl.ds(128 * n, 128), :] = src[at]
            catt[:, pl.ds(128 * n, 128)] = srct[at]
            source = bar - offset
            length = len_ref[0, jnp.maximum(source, 0)]
            lens.append(jnp.where(source >= 0, length, 0))

        qg = qgr[i]
        none = jnp.zeros_like(qg)
        b_ref[pl.ds(0, 128), :] = jnp.where(left, qg, none)
        b_ref[pl.ds(128, 128), :] = jnp.where(left, none, qg)
        s_ref[...] = dot_nt(cat[...], b_ref[...])

        spans = [(128 * n, 128) for n in range(9)] + [(1152, 64)]
        top = jnp.full((8, BAR), LOW, F32)
        for n, (at, size) in enumerate(spans):
            s = s_ref[pl.ds(at, size), 0:128]
            if n == 0:
                keep = (row <= col) & (row < lens[0])
            elif n < 9:
                keep = row < lens[n]
            else:
                keep = sbar < bar
            s = jnp.where(keep, s, LOW)
            s_ref[pl.ds(at, size), 0:128] = s
            top = jnp.maximum(top, jnp.max(s.reshape(size // 8, 8, BAR), axis=0))
        top = jnp.max(top, axis=0, keepdims=True)
        total = jnp.zeros((8, BAR), F32)
        for at, size in spans:
            e = jnp.exp(s_ref[pl.ds(at, size), 0:128] - top)
            s_ref[pl.ds(at, size), 0:128] = e
            total = total + jnp.sum(e.reshape(size // 8, 8, BAR), axis=0)
        inv = 1.0 / jnp.sum(total, axis=0, keepdims=True)
        delta = jnp.zeros((8, BAR), F32)
        for at, size in spans:
            prob = s_ref[pl.ds(at, size), 0:128] * inv
            pb = prob.astype(BF)
            x_ref[pl.ds(at, size), 128:256] = pb
            term = pb.astype(F32) * s_ref[pl.ds(at, size), 128:256]
            delta = delta + jnp.sum(term.reshape(size // 8, 8, BAR), axis=0)
        delta = jnp.sum(delta, axis=0, keepdims=True)
        for at, size in spans:
            prob = s_ref[pl.ds(at, size), 0:128] * inv
            ds = prob * (s_ref[pl.ds(at, size), 128:256] - delta)
            x_ref[pl.ds(at, size), 0:128] = ds.astype(BF)

        out = dot(catt[...], x_ref[...])
        dqs[i] = (out[0:HEAD, 0:128] * 0.125).astype(BF)
        ats[i] = out[HEAD:128, 128:256].astype(BF)

        half = lax.div(i0, 8)
        slot = lax.rem(i0, 8)

        @pl.when(i != i0)
        def _():
            remote(dqs.at[i], dqr.at[i0], dq_s.at[i], dq_rs.at[i0], peer(i)).start()

        @pl.when(i == i0)
        def _():
            dqr[i] = dqs[i]

        here = jnp.logical_and(i == i0, core == half)

        @pl.when(jnp.logical_not(here))
        def _():
            remote(ats.at[i], atr.at[core, slot], at_s.at[i], at_rs.at[core, slot], near(i, half)).start()

        @pl.when(here)
        def _():
            atr[core, slot] = ats[i]

        rhs = b_ref[...]
        for n, (src, _, at, offset) in enumerate(blocks):
            term = dot(x_ref[pl.ds(128 * n, 128), :], rhs)
            if n == 1:
                d1s[i] = term.astype(BF)
                remote(d1s.at[i], d1r.at[i], d1_s.at[i], d1_rs.at[i], sib).start()
            elif n == 2:
                d2f[lax.rem(i, 2)] = term

                @pl.when(even)
                def _():
                    d2s[i] = term.astype(BF)
                    remote(d2s.at[i], d2r.at[i], d2_s.at[i], d2_rs.at[i], far).start()
            else:
                acc[at] += term
        accsum[...] += dot(x_ref[pl.ds(1152, 64), :], rhs).reshape(4, 16, BAR)

        @pl.when(i > 0)
        def _():
            join(i - 1)

    loop(0, N, one_bar)

    for device, rr in others:
        remote(accsum.at[rr], sgr.at[r], sg_s.at[rr], sg_rs.at[r], device).start()
    join(N - 1)

    remote(do2.at[1 - core], do2.at[1 - core], do_s.at[0], do_r.at[0], sib).wait_recv()

    def get_attn(h):
        head = 8 * core + h
        for c in range(2):
            @pl.when(jnp.logical_not(jnp.logical_and(head == i0, core == c)))
            def _():
                remote(ats.at[0], atr.at[c, h], at_s.at[0], at_rs.at[c, h], sib).wait_recv()

    loop(0, 8, get_attn)

    def project(t):
        lhs = jnp.concatenate(
            [atr[0, pl.ds(2 * t, 2)].reshape(128, BAR), atr[1, pl.ds(2 * t, 2)].reshape(128, BAR)], axis=1
        )
        part = dot(lhs, do2[...].reshape(256, WIDTH)).astype(BF)
        dws[pl.ds(2 * t, 2)] = part.reshape(2, 2, 2, 16, WIDTH)
        for u in range(2):
            h = 2 * t + u
            head = 8 * core + h
            remote(
                dws.at[h, :, 1 - core], dwr.at[i0], dw_s.at[h, 1 - core], dw_rs.at[i0], near(head, 1 - core)
            ).start()

            @pl.when(head != i0)
            def _():
                remote(dws.at[h, :, core], dwr.at[i0], dw_s.at[h, core], dw_rs.at[i0], peer(head)).start()

            @pl.when(head == i0)
            def _():
                dwr[i0] = dws[h, :, core]

    loop(0, 4, project)

    for device, rr in others:
        remote(accsum.at[rr], sgr.at[rr], sg_s.at[rr], sg_rs.at[rr], device).wait_recv()
    sgr[r] = accsum[r]
    sumf[...] = sgr[0] + sgr[1] + sgr[2] + sgr[3]
    back = jnp.where(r >= 2, 1, 0)

    def gather_terms(i):
        remote(d2s.at[i], d2r.at[i], d2_s.at[i], d2_rs.at[i], far).wait_recv()
        acc[PAD + i - back] += d2r[i].astype(F32)

        @pl.when(even)
        def _():
            remote(d1s.at[i], d1r.at[i], d1_s.at[i], d1_rs.at[i], sib).wait_recv()
            acc[PAD + i] += d1r[i].astype(F32)

    loop(0, N, gather_terms)

    def finish(d):
        j = rot(d)
        spot = spot_ref[0, 4 * j + r]
        extra = jnp.where(row == spot, sumf[pl.ds(j, 1), :], 0.0)
        fks[j] = (acc[PAD + j] + extra).astype(BF)

        @pl.when(d > 0)
        def _():
            remote(fks.at[j], fkr.at[i0], fk_s.at[j], fk_rs.at[i0], peer(j)).start()

    loop(0, N, finish)
    fkr[i0] = fks[i0]

    def get_dw(j):
        @pl.when(jnp.logical_not(jnp.logical_and(j == i0, core == lax.div(i0, 8))))
        def _():
            remote(dws.at[0, :, 0], dwr.at[j], dw_s.at[0, 0], dw_rs.at[j], sib).wait_recv()

    loop(0, N, get_dw)
    for a in range(2):
        part = dwr[0, a].astype(F32)
        for j in range(1, N):
            part = part + dwr[j, a].astype(F32)
        wsum[a] = part
        zs[a] = part.astype(BF)

    def send_z(d):
        t = lax.rem(z + d, 8)
        remote(zs.at[lax.div(t, 4)], zr.at[z], z_s.at[t], z_rs.at[z], zpeer(t)).start()

    loop(1, 8, send_z)

    def get_dq(d):
        j = rot(d)
        remote(dqs.at[j], dqr.at[j], dq_s.at[j], dq_rs.at[j], peer(j)).wait_recv()

    loop(1, N, get_dq)
    for p in range(N // 2):
        dq_ref[:, 128 * p : 128 * p + 128] = dqr[2 * p : 2 * p + 2].reshape(128, 128).T

    def get_fk(d):
        j = rot(d)
        remote(fks.at[j], fkr.at[j], fk_s.at[j], fk_rs.at[j], peer(j)).wait_recv()

    loop(1, N, get_fk)
    for p in range(N // 2):
        cols = slice(128 * p, 128 * p + 128)
        a = fkr[2 * p]
        b = fkr[2 * p + 1]
        dk_ref[:, cols] = jnp.concatenate([a[:, :HEAD], b[:, :HEAD]], axis=1)
        dv_ref[:, cols] = jnp.concatenate([a[:, HEAD:], b[:, HEAD:]], axis=1)

    def get_z(d):
        t = lax.rem(z + d, 8)
        remote(zs.at[0], zr.at[t], z_s.at[t], z_rs.at[t], zpeer(t)).wait_recv()

    loop(1, 8, get_z)
    zr[z] = zs[zh]
    whole = wsum[zh]

    def add_z(d, total):
        return total + zr[lax.rem(z + d, 8)].astype(F32)

    dw_ref[...] = lax.fori_loop(1, 8, add_z, whole)

    wa.wait_send()
    do_copy.wait_send()

    def drain(d):
        j = rot(d)
        remote(kvs.at[j], kvo.at[PAD + i0], kv_s.at[j], kv_r.at[i0], peer(j)).wait_send()
        remote(w4.at[i0, :, core], w4.at[i0, :, core], wb_s.at[j], wb_r.at[i0], peer(j)).wait_send()
        remote(qgs.at[j], qgr.at[i0], qg_s.at[j], qg_r.at[i0], peer(j)).wait_send()
        remote(dqs.at[j], dqr.at[i0], dq_s.at[j], dq_rs.at[i0], peer(j)).wait_send()
        remote(fks.at[j], fkr.at[i0], fk_s.at[j], fk_rs.at[i0], peer(j)).wait_send()

    loop(1, N, drain)

    def drain_all(j):
        remote(kvo.at[PAD + j], p2.at[1 + j], p2_s.at[j], p2_r.at[j], far).wait_send()
        remote(kvo.at[PAD + j], p1.at[1 + j], p1_s.at[j], p1_r.at[j], sib).wait_send()
        remote(w4.at[j, :, core], w4.at[j, :, core], wc_s.at[j], wc_r.at[j], sib).wait_send()
        remote(d1s.at[j], d1r.at[j], d1_s.at[j], d1_rs.at[j], sib).wait_send()
        remote(d2s.at[j], d2r.at[j], d2_s.at[j], d2_rs.at[j], far).wait_send()

        @pl.when(jnp.logical_not(jnp.logical_and(j == i0, core == lax.div(i0, 8))))
        def _():
            remote(ats.at[j], atr.at[0, 0], at_s.at[j], at_rs.at[0, 0], sib).wait_send()

    loop(0, N, drain_all)

    def drain_w(h):
        head = 8 * core + h
        remote(dws.at[h, :, 1 - core], dwr.at[i0], dw_s.at[h, 1 - core], dw_rs.at[i0], sib).wait_send()

        @pl.when(head != i0)
        def _():
            remote(dws.at[h, :, core], dwr.at[i0], dw_s.at[h, core], dw_rs.at[i0], peer(head)).wait_send()

    loop(0, 8, drain_w)

    def drain_z(d):
        t = lax.rem(z + d, 8)
        remote(zs.at[lax.div(t, 4)], zr.at[z], z_s.at[t], z_rs.at[z], zpeer(t)).wait_send()

    loop(1, 8, drain_z)
    for device, rr in others:
        remote(sumkv.at[r], sumkv.at[r], sm_s.at[rr], sm_r.at[r], device).wait_send()
        remote(accsum.at[rr], sgr.at[r], sg_s.at[rr], sg_rs.at[r], device).wait_send()


def on_device(queries, keys, values, d_out, out_weight, bar_lengths, summary_pos):
    vm = pltpu.VMEM
    dma = pltpu.SemaphoreType.DMA
    blocks = lambda n, kind=BF: vm((n, BAR, BAR), kind)
    scratch = [
        blocks(N), blocks(PAD + N), blocks(1 + N), blocks(1 + N),
        blocks(PAD + N), blocks(1 + N), blocks(1 + N),
        blocks(N), blocks(N),
        vm((N, 2, 2, 16, WIDTH), BF), vm((2, BAR, WIDTH), BF),
        vm((16, BAR), F32), vm((4, 16, BAR), BF), vm((BAR, BAR), BF),
        vm((256, BAR), BF), vm((NKEYS, 256), F32), vm((NKEYS, 256), BF),
        vm((NKEYS, BAR), BF), vm((BAR, NKEYS), BF),
        blocks(PAD + N, F32), vm((4, 16, BAR), F32),
        blocks(N), blocks(N), blocks(N), blocks(N), blocks(2, F32), vm((4, 16, BAR), F32),
        blocks(N), blocks(N),
        vm((N, HEAD, BAR), BF), vm((N, HEAD, BAR), BF),
        vm((N, HEAD, BAR), BF), vm((2, 8, HEAD, BAR), BF),
        vm((8, 2, 2, 16, WIDTH), BF), vm((N, 2, 16, WIDTH), BF),
        vm((2, 16, WIDTH), F32), vm((2, 16, WIDTH), BF), vm((8, 16, WIDTH), BF),
    ]
    sems = [(N,)] * 6 + [(1,)] * 2 + [(N,)] * 4 + [(1,)] * 2 + [(N,)] * 2 + [(4,)] * 2
    sems += [(N,)] * 4 + [(4,)] * 2 + [(N,)] * 4 + [(N,), (2, 8), (8, 2), (N,), (8,), (8,)]
    scratch += [dma(shape) for shape in sems]
    in_vmem = pl.BlockSpec(memory_space=pltpu.VMEM)
    in_smem = pl.BlockSpec(memory_space=pltpu.SMEM)
    rows = jax.ShapeDtypeStruct((BAR, WIDTH), BF)
    d_q, d_k, d_v, d_w = pl.pallas_call(
        kernel,
        out_shape=(rows, rows, rows, jax.ShapeDtypeStruct((16, WIDTH), F32)),
        in_specs=[in_vmem] * 5 + [in_smem] * 2,
        out_specs=(in_vmem,) * 4,
        scratch_shapes=scratch,
        compiler_params=pltpu.CompilerParams(
            collective_id=0, has_side_effects=True, vmem_limit_bytes=48 * 1024 * 1024
        ),
    )(queries[0, 0], keys[0, 0], values[0, 0], d_out[0, 0], out_weight, bar_lengths, summary_pos)
    return d_q[None, None], d_k[None, None], d_v[None, None], d_w


def solution(mesh):
    spread = P("dp", "ctx", None, None)
    return jax.shard_map(
        on_device,
        mesh=mesh,
        in_specs=(spread,) * 4 + (P("ctx", None), P("dp", None), P("dp", None)),
        out_specs=(spread,) * 3 + (P("ctx", None),),
        check_vma=False,
    )
```

time: 1880 us -> 115 us (0.06)
  the two profiles are of different devices: /device:TPU:2 before, /device:TPU:14 now
where the time goes in v1:
time: 115 us
  Pallas kernels  106 us (92%)
  local copies, waits for them, and re-layouts  7.95 us (7%)
    pallas_call x1, Pallas kernels, on_device(): pl.pallas_call(kernel, out_shape=(rows, rows, rows, jax.ShapeDtypeStruct(...  106 us
    unnamed x18, local copies, waits for them, and re-layouts  7.95 us

profile of v1, /device:TPU:14, one launch (start us, length us, event | category | flops | bytes accessed | tf_op | source)
XLA Modules:
  0.0 114.8 jit_solution(17612715156399517906)
XLA Ops:
  0.6 0.0 copy-start.5
  0.6 0.0 copy-start.6
  0.7 0.6 copy-done.5
  1.3 0.0 copy-done.6
  1.3 0.0 copy-start
  1.3 0.9 copy-done
  2.3 0.0 copy-start.1
  2.3 0.9 copy-done.1
  3.2 0.0 copy-start.2
  3.2 0.9 copy-done.2
  4.2 0.0 copy-start.3
  4.2 0.9 copy-done.3
  5.1 0.0 copy-start.4
  5.1 0.8 copy-done.4
  5.9 106.2 %shard_map.102 = (bf16[128,1024]{1,0:T(8,128)(2,1)S(1)}, bf16[128,1024]{1,0:T(8,128)(2,1)S(1)}, bf16[128,1024]{1,0:T(8,128)(2,1)S(1)}, f32[16,1024]{1,0:T(8,128)S(1)}) custom-call(bf16[128,1024]{1,0:T(8,128)(2,1)S(1)} %bitcast.7, bf16[128,1024]{1,0:T(8,128)(2,1)S(1)} %bitcast.8, bf16[128,1024]{1,0:T(8,128)(2,1)S(1)} %bitcast.9, ...), custom_call_target="tpu_custom_call" | custom-call | tf_op jit(solution)/shard_map/pallas_call | solution.py:512
  112.1 0.7 copy.15
  112.8 0.7 copy.16
  113.5 0.7 copy.17
  114.2 0.6 copy.18
Async XLA Ops:
  0.6 0.7 copy-start.5
  0.6 0.7 copy-start.6
  1.3 0.9 copy-start
  2.3 0.9 copy-start.1
  3.2 0.9 copy-start.2
  4.2 0.9 copy-start.3
  5.1 0.8 copy-start.4

commit v2 on v1

v2 whole, which is shorter than its diff:
```python
import jax
import jax.numpy as jnp
from jax import lax
from jax.experimental import pallas as pl
from jax.experimental.pallas import tpu as pltpu
from jax.sharding import PartitionSpec as P

N = 16
BAR = 128
HEAD = 64
WIDTH = 1024
PAD = 8
NKEYS = 1280
OWN_STEPS = (1, 2, 3, 4, 6, 8)
AHEAD = 6
LAG_J = 2
LAG = 6
LAG_P = 4
LAG_W = 8
LOW = -1e30
MESH = pl.DeviceIdType.MESH
BF = jnp.bfloat16
F32 = jnp.float32


def remote(src, dst, send, recv, device):
    return pltpu.make_async_remote_copy(
        src_ref=src, dst_ref=dst, send_sem=send, recv_sem=recv, device_id=device, device_id_type=MESH
    )


def loop(low, high, body):
    def step(i, carry):
        body(i)
        return carry

    lax.fori_loop(low, high, step, 0)


def dot_nt(a, b):
    return lax.dot_general(a, b, (((1,), (1,)), ((), ())), preferred_element_type=F32)


def dot(a, b):
    return jnp.dot(a, b, preferred_element_type=F32)


def kernel(
    q_hbm, k_hbm, v_hbm, do_hbm, w_hbm, len_ref, spot_ref,
    dq_ref, dk_ref, dv_ref, dw_ref,
    q_ref, k_ref, v_ref, kvs, kvo, p1, p2, kvot, p1t, p2t, qgs, qgr, w4, do2, sumf, sumkv, sumt,
    b_ref, s_ref, x_ref, cat, catt, acc, accsum, d1s, d1r, d2s, d2r, d2f, sgr,
    fks, fkr, dqs, dqr, ats, atr, dws, dwr, wsum, zs, zr,
    in_s, kv_s, kv_r, p1_s, p1_r, p2_s, p2_r, wa_s, wa_r, wb_s, wb_r, wc_s, wc_r, do_s, do_r,
    qg_s, qg_r, sm_s, sm_r, d1_s, d1_rs, d2_s, d2_rs, sg_s, sg_rs, fk_s, fk_rs,
    dq_s, dq_rs, at_s, at_rs, dw_s, dw_rs, z_s, z_rs,
):
    dp = lax.axis_index("dp")
    ctx = lax.axis_index("ctx")
    i0 = lax.div(ctx, 4)
    r = lax.rem(ctx, 4)
    zh = lax.div(r, 2)
    core = lax.rem(r, 2)
    z = zh * 4 + dp
    odd = core == 1
    even = core == 0
    me = (dp, ctx)
    sib = (dp, 4 * i0 + 2 * zh + (1 - core))
    far = (dp, 4 * i0 + 2 * (1 - zh) + core)
    diag = (dp, 4 * i0 + 2 * (1 - zh) + (1 - core))

    def peer(j):
        return (dp, 4 * j + r)

    def near(j, c):
        return (dp, 4 * j + 2 * zh + c)

    def zpeer(t):
        return (lax.rem(t, 4), 4 * i0 + 2 * lax.div(t, 4) + core)

    def rot(d):
        return lax.rem(i0 + d, N)

    loads = [
        pltpu.make_async_copy(k_hbm, k_ref, in_s.at[0]),
        pltpu.make_async_copy(v_hbm, v_ref, in_s.at[1]),
        pltpu.make_async_copy(w_hbm, w4.at[i0, zh, core], in_s.at[2]),
        pltpu.make_async_copy(do_hbm, do2.at[core], in_s.at[3]),
        pltpu.make_async_copy(q_hbm, q_ref, in_s.at[4]),
    ]
    for load in loads:
        load.start()

    barrier = pltpu.get_barrier_semaphore()

    def greet(device):
        pl.semaphore_signal(barrier, inc=1, device_id=device, device_id_type=MESH)

    loop(0, N, lambda d: greet(near(rot(d), 1 - core)))
    loop(1, N, lambda d: greet(peer(rot(d))))
    loop(1, 8, lambda d: greet(zpeer(lax.rem(z + d, 8))))
    greet(diag)

    loads[0].wait()
    loads[1].wait()
    for p in range(N // 2):
        cols = slice(128 * p, 128 * p + 128)
        kk = k_ref[:, cols]
        vv = v_ref[:, cols]
        kvs[2 * p] = jnp.concatenate([kk[:, :HEAD], vv[:, :HEAD]], axis=1)
        kvs[2 * p + 1] = jnp.concatenate([kk[:, HEAD:], vv[:, HEAD:]], axis=1)
    kvo[PAD + i0] = kvs[i0]
    loads[2].wait()
    loads[3].wait()
    loads[4].wait()
    pl.semaphore_wait(barrier, 39)

    wa = remote(w4.at[i0, zh, core], w4.at[i0, zh, core], wa_s.at[0], wa_r.at[0], far)
    wa.start()

    def send_kv(d):
        j = rot(d)
        remote(kvs.at[j], kvo.at[PAD + i0], kv_s.at[j], kv_r.at[i0], peer(j)).start()

    loop(1, N, send_kv)
    do_copy = remote(do2.at[core], do2.at[core], do_s.at[0], do_r.at[0], sib)
    do_copy.start()
    remote(w4.at[i0, 1 - zh, core], w4.at[i0, 1 - zh, core], wa_s.at[0], wa_r.at[0], far).wait_recv()

    def send_w(d):
        j = rot(d)
        remote(w4.at[i0, :, core], w4.at[i0, :, core], wb_s.at[j], wb_r.at[i0], peer(j)).start()

    loop(1, N, send_w)

    zero = jnp.zeros((BAR, BAR), BF)
    for n in range(PAD):
        kvo[n] = zero
        kvot[n] = zero
    p1[0] = zero
    p1t[0] = zero
    p2[0] = zero
    p2t[0] = zero
    cat[pl.ds(0, 128), :] = zero
    x_ref[pl.ds(0, 128), :] = jnp.zeros((128, 256), BF)
    acc[...] = jnp.zeros(acc.shape, F32)
    accsum[...] = jnp.zeros(accsum.shape, F32)
    wsum[...] = jnp.zeros(wsum.shape, F32)

    row = lax.broadcasted_iota(jnp.int32, (BAR, BAR), 0)
    col = lax.broadcasted_iota(jnp.int32, (BAR, BAR), 1)

    def pass_on(d):
        j = lax.rem(i0 - d + N, N)

        @pl.when(d > 0)
        def _():
            remote(kvs.at[j], kvo.at[PAD + j], kv_s.at[j], kv_r.at[j], peer(j)).wait_recv()

        remote(kvo.at[PAD + j], p2.at[1 + j], p2_s.at[j], p2_r.at[j], far).start()

        @pl.when(even)
        def _():
            remote(kvo.at[PAD + j], p1.at[1 + j], p1_s.at[j], p1_r.at[j], sib).start()

        block = kvo[PAD + j]
        kvot[PAD + j] = block.T
        spot = spot_ref[0, 4 * j + r]
        picked = jnp.where(row == spot, block.astype(F32), 0.0)
        sumf[pl.ds(j, 1), :] = jnp.sum(picked, axis=0, keepdims=True)

    loop(0, N, pass_on)
    sumkv[r] = sumf[...].astype(BF)
    r_sib = 2 * zh + (1 - core)
    r_far = 2 * (1 - zh) + core
    r_diag = 2 * (1 - zh) + (1 - core)
    others = ((sib, r_sib), (far, r_far), (diag, r_diag))
    for device, rr in others:
        remote(sumkv.at[r], sumkv.at[r], sm_s.at[rr], sm_r.at[r], device).start()

    def pass_w(d):
        j = rot(d)

        @pl.when(d > 0)
        def _():
            remote(w4.at[j, :, core], w4.at[j, :, core], wb_s.at[j], wb_r.at[j], peer(j)).wait_recv()

        remote(w4.at[j, :, core], w4.at[j, :, core], wc_s.at[j], wc_r.at[j], sib).start()

    loop(0, N, pass_w)

    for c in range(4):
        line = lax.rem(lax.div(i0, 4) + c, 4)
        for n in range(4):
            j = 4 * line + n
            remote(w4.at[j, :, 1 - core], w4.at[j, :, 1 - core], wc_s.at[j], wc_r.at[j], sib).wait_recv()
        rows = w4[pl.ds(4 * line, 4)].reshape(256, WIDTH)
        g = dot_nt(do2[core], rows).astype(BF)
        qq = q_ref[:, pl.ds(pl.multiple_of(256 * line, 256), 256)]
        qq = (qq.astype(F32) * 0.125).astype(BF)
        for n in range(4):
            cols = slice(HEAD * n, HEAD * n + HEAD)
            qgs[4 * line + n] = jnp.concatenate([qq[:, cols], g[:, cols]], axis=1)
        for n in range(4):
            h = 4 * line + lax.rem(i0 + n, 4)

            @pl.when(i0 != h)
            def _():
                remote(qgs.at[h], qgr.at[i0], qg_s.at[h], qg_r.at[i0], peer(h)).start()

    qgr[i0] = qgs[i0]

    for device, rr in others:
        remote(sumkv.at[rr], sumkv.at[rr], sm_s.at[rr], sm_r.at[rr], device).wait_recv()
    cat[pl.ds(0, 64), :] = sumkv[...].reshape(64, BAR)
    catt[:, pl.ds(0, 128)] = cat[pl.ds(0, 128), :].T

    def behind(t):
        return lax.rem(i0 - t + N, N)

    def take_far(t):
        j = behind(t)
        remote(kvo.at[PAD + j], p2.at[1 + j], p2_s.at[j], p2_r.at[j], far).wait_recv()

        @pl.when(odd)
        def _():
            remote(p2.at[1 + j], p1.at[1 + j], p1_s.at[j], p1_r.at[j], sib).start()

        p2t[1 + j] = p2[1 + j].T

    def take_near(t):
        j = behind(t)
        remote(kvo.at[PAD + j], p1.at[1 + j], p1_s.at[j], p1_r.at[j], sib).wait_recv()
        p1t[1 + j] = p1[1 + j].T

    loop(0, AHEAD, take_far)
    loop(0, AHEAD - 2, take_near)

    lag1 = jnp.where(r < 1, 1, 0)
    lag2 = jnp.where(r < 2, 1, 0)
    srow = lax.broadcasted_iota(jnp.int32, (64, BAR), 0)
    sbar = 4 * lax.rem(srow, 16) + lax.div(srow, 16)
    left = col < HEAD

    half = lax.rem(i0, 2)
    slot = lax.div(i0, 2)

    def send_far(i):
        @pl.when(jnp.logical_or(zh == 1, i > 0))
        def _():
            remote(d2s.at[i], d2r.at[i], d2_s.at[i], d2_rs.at[i], far).start()

    def join(i):
        @pl.when(odd)
        def _():
            remote(d1s.at[i], d1r.at[i], d1_s.at[i], d1_rs.at[i], sib).wait_recv()
            d2s[i] = (d2f[lax.rem(i, 4)] + d1r[i].astype(F32)).astype(BF)
            send_far(i)

    def take_terms(t):
        at = behind(t)

        @pl.when(jnp.logical_or(zh == 0, at > 0))
        def _():
            remote(d2s.at[at], d2r.at[at], d2_s.at[at], d2_rs.at[at], far).wait_recv()
            acc[PAD + at - zh] += d2r[at].astype(F32)

        @pl.when(even)
        def _():
            remote(d1s.at[at], d1r.at[at], d1_s.at[at], d1_rs.at[at], sib).wait_recv()
            acc[PAD + at] += d1r[at].astype(F32)

    def project(t):
        head = rot(t)

        @pl.when(lax.rem(head, 2) == core)
        def _():
            at = lax.div(head, 2)
            for c in range(2):
                @pl.when(jnp.logical_not(jnp.logical_and(t == 0, core == c)))
                def _():
                    remote(ats.at[0], atr.at[c, at], at_s.at[0], at_rs.at[c, at], sib).wait_recv()

            lhs = jnp.concatenate([atr[0, at], atr[1, at]], axis=1)
            part = dot(lhs, do2[...].reshape(256, WIDTH)).astype(BF)
            dws[at] = part.reshape(2, 2, 16, WIDTH)
            remote(
                dws.at[at, :, 1 - core], dwr.at[i0], dw_s.at[at, 1 - core], dw_rs.at[i0], near(head, 1 - core)
            ).start()

            @pl.when(t > 0)
            def _():
                remote(dws.at[at, :, core], dwr.at[i0], dw_s.at[at, core], dw_rs.at[i0], peer(head)).start()

            @pl.when(t == 0)
            def _():
                dwr[i0] = dws[at, :, core]

    def take_dw(t):
        j = behind(t)

        @pl.when(jnp.logical_not(jnp.logical_and(t == 0, core == half)))
        def _():
            remote(dws.at[0, :, 0], dwr.at[j], dw_s.at[0, 0], dw_rs.at[j], sib).wait_recv()

        wsum[...] += dwr[j].astype(F32)

    remote(do2.at[1 - core], do2.at[1 - core], do_s.at[0], do_r.at[0], sib).wait_recv()

    def attend(i, steps):
        bar = 4 * i + r
        blocks = [(kvo, kvot, PAD + i, 0), (p1, p1t, 1 + i - lag1, 1), (p2, p2t, 1 + i - lag2, 2)]
        blocks += [(kvo, kvot, PAD + i - m, 4 * m) for m in steps]
        lens = []
        for n, (src, srct, at, offset) in enumerate(blocks):
            cat[pl.ds(128 * n + 128, 128), :] = src[at]
            catt[:, pl.ds(128 * n + 128, 128)] = srct[at]
            source = bar - offset
            length = len_ref[0, jnp.maximum(source, 0)]
            lens.append(jnp.where(source >= 0, length, 0))

        qg = qgr[i]
        none = jnp.zeros_like(qg)
        b_ref[pl.ds(0, 128), :] = jnp.where(left, qg, none)
        b_ref[pl.ds(128, 128), :] = jnp.where(left, none, qg)
        size_all = 128 * len(blocks) + 128
        s_ref[pl.ds(0, size_all), :] = dot_nt(cat[pl.ds(0, size_all), :], b_ref[...])

        spans = [(128 * n + 128, 128) for n in range(len(blocks))] + [(0, 64)]
        top = jnp.full((8, BAR), LOW, F32)
        for n, (at, size) in enumerate(spans):
            s = s_ref[pl.ds(at, size), 0:128]
            if n == 0:
                keep = (row <= col) & (row < lens[0])
            elif n < len(blocks):
                keep = row < lens[n]
            else:
                keep = sbar < bar
            s = jnp.where(keep, s, LOW)
            s_ref[pl.ds(at, size), 0:128] = s
            top = jnp.maximum(top, jnp.max(s.reshape(size // 8, 8, BAR), axis=0))
        top = jnp.max(top, axis=0, keepdims=True)
        total = jnp.zeros((8, BAR), F32)
        for at, size in spans:
            e = jnp.exp(s_ref[pl.ds(at, size), 0:128] - top)
            s_ref[pl.ds(at, size), 0:128] = e
            total = total + jnp.sum(e.reshape(size // 8, 8, BAR), axis=0)
        inv = 1.0 / jnp.sum(total, axis=0, keepdims=True)
        delta = jnp.zeros((8, BAR), F32)
        for at, size in spans:
            prob = s_ref[pl.ds(at, size), 0:128] * inv
            pb = prob.astype(BF)
            x_ref[pl.ds(at, size), 128:256] = pb
            term = pb.astype(F32) * s_ref[pl.ds(at, size), 128:256]
            delta = delta + jnp.sum(term.reshape(size // 8, 8, BAR), axis=0)
        delta = jnp.sum(delta, axis=0, keepdims=True)
        for at, size in spans:
            prob = s_ref[pl.ds(at, size), 0:128] * inv
            ds = prob * (s_ref[pl.ds(at, size), 128:256] - delta)
            x_ref[pl.ds(at, size), 0:128] = ds.astype(BF)

        out = dot(catt[:, pl.ds(0, size_all)], x_ref[pl.ds(0, size_all), :])
        dqs[i] = (out[0:HEAD, 0:128] * 0.125).astype(BF)
        ats[i] = out[HEAD:128, 128:256].astype(BF)

        rhs = b_ref[...]
        for n, (src, _, at, offset) in enumerate(blocks):
            term = dot(x_ref[pl.ds(128 * n + 128, 128), :], rhs)
            if n == 1:
                d1s[i] = term.astype(BF)
                remote(d1s.at[i], d1r.at[i], d1_s.at[i], d1_rs.at[i], sib).start()
            elif n == 2:
                d2f[lax.rem(i, 4)] = term

                @pl.when(even)
                def _():
                    d2s[i] = term.astype(BF)
                    send_far(i)
            else:
                acc[at] += term
        accsum[...] += dot(x_ref[pl.ds(0, 64), :], rhs)

    def one_bar(t):
        i = behind(t)

        @pl.when(t + AHEAD < N)
        def _():
            take_far(t + AHEAD)

        @pl.when(t + AHEAD - 2 < N)
        def _():
            take_near(t + AHEAD - 2)

        @pl.when(i != i0)
        def _():
            remote(qgs.at[i], qgr.at[i], qg_s.at[i], qg_r.at[i], peer(i)).wait_recv()


        @pl.when(i >= 8)
        def _():
            attend(i, OWN_STEPS)

        @pl.when(jnp.logical_and(i >= 4, i < 8))
        def _():
            attend(i, OWN_STEPS[:5])

        @pl.when(i < 4)
        def _():
            attend(i, OWN_STEPS[:3])

        @pl.when(i != i0)
        def _():
            remote(dqs.at[i], dqr.at[i0], dq_s.at[i], dq_rs.at[i0], peer(i)).start()

        @pl.when(i == i0)
        def _():
            dqr[i] = dqs[i]

        here = jnp.logical_and(i == i0, core == half)

        @pl.when(jnp.logical_not(here))
        def _():
            remote(ats.at[i], atr.at[core, slot], at_s.at[i], at_rs.at[core, slot], near(i, half)).start()

        @pl.when(here)
        def _():
            atr[core, slot] = ats[i]

        @pl.when(t >= LAG_J)
        def _():
            join(behind(t - LAG_J))

        @pl.when(t >= LAG_P)
        def _():
            project(t - LAG_P)

        @pl.when(t >= LAG)
        def _():
            take_terms(t - LAG)

        @pl.when(t >= LAG_W)
        def _():
            take_dw(t - LAG_W)

    loop(0, N, one_bar)
    loop(N - LAG_J, N, lambda t: join(behind(t)))
    for device, rr in others:
        remote(accsum.at[pl.ds(16 * rr, 16)], sgr.at[r], sg_s.at[rr], sg_rs.at[r], device).start()
    loop(N - LAG_P, N, project)
    loop(N - LAG, N, take_terms)

    for device, rr in others:
        remote(sgr.at[rr], sgr.at[rr], sg_s.at[rr], sg_rs.at[rr], device).wait_recv()
    sgr[r] = accsum[pl.ds(16 * r, 16), :]
    sumf[...] = sgr[0] + sgr[1] + sgr[2] + sgr[3]

    def finish(d):
        j = rot(d)
        spot = spot_ref[0, 4 * j + r]
        extra = jnp.where(row == spot, sumf[pl.ds(j, 1), :], 0.0)
        fks[j] = (acc[PAD + j] + extra).astype(BF)

        @pl.when(d > 0)
        def _():
            remote(fks.at[j], fkr.at[i0], fk_s.at[j], fk_rs.at[i0], peer(j)).start()

    loop(0, N, finish)
    fkr[i0] = fks[i0]

    loop(N - LAG_W, N, take_dw)
    zs[...] = wsum[...].astype(BF)

    def send_z(d):
        t = lax.rem(z + d, 8)
        remote(zs.at[lax.div(t, 4)], zr.at[z], z_s.at[t], z_rs.at[z], zpeer(t)).start()

    loop(1, 8, send_z)

    def get_dq(d):
        j = rot(d)
        remote(dqs.at[j], dqr.at[j], dq_s.at[j], dq_rs.at[j], peer(j)).wait_recv()

    loop(1, N, get_dq)
    for p in range(N // 2):
        dq_ref[:, 128 * p : 128 * p + 128] = dqr[2 * p : 2 * p + 2].reshape(128, 128).T

    def get_fk(d):
        j = rot(d)
        remote(fks.at[j], fkr.at[j], fk_s.at[j], fk_rs.at[j], peer(j)).wait_recv()

    loop(1, N, get_fk)
    for p in range(N // 2):
        cols = slice(128 * p, 128 * p + 128)
        a = fkr[2 * p]
        b = fkr[2 * p + 1]
        dk_ref[:, cols] = jnp.concatenate([a[:, :HEAD], b[:, :HEAD]], axis=1)
        dv_ref[:, cols] = jnp.concatenate([a[:, HEAD:], b[:, HEAD:]], axis=1)

    def get_z(d):
        t = lax.rem(z + d, 8)
        remote(zs.at[0], zr.at[t], z_s.at[t], z_rs.at[t], zpeer(t)).wait_recv()

    loop(1, 8, get_z)
    zr[z] = zs[zh]
    whole = wsum[zh]

    def add_z(d, total):
        return total + zr[lax.rem(z + d, 8)].astype(F32)

    dw_ref[...] = lax.fori_loop(1, 8, add_z, whole)

    wa.wait_send()
    do_copy.wait_send()

    def drain(d):
        j = rot(d)
        remote(kvs.at[j], kvo.at[PAD + i0], kv_s.at[j], kv_r.at[i0], peer(j)).wait_send()
        remote(w4.at[i0, :, core], w4.at[i0, :, core], wb_s.at[j], wb_r.at[i0], peer(j)).wait_send()
        remote(qgs.at[j], qgr.at[i0], qg_s.at[j], qg_r.at[i0], peer(j)).wait_send()
        remote(dqs.at[j], dqr.at[i0], dq_s.at[j], dq_rs.at[i0], peer(j)).wait_send()
        remote(fks.at[j], fkr.at[i0], fk_s.at[j], fk_rs.at[i0], peer(j)).wait_send()

    loop(1, N, drain)

    def drain_all(j):
        remote(kvo.at[PAD + j], p2.at[1 + j], p2_s.at[j], p2_r.at[j], far).wait_send()
        remote(kvo.at[PAD + j], p1.at[1 + j], p1_s.at[j], p1_r.at[j], sib).wait_send()
        remote(w4.at[j, :, core], w4.at[j, :, core], wc_s.at[j], wc_r.at[j], sib).wait_send()
        remote(d1s.at[j], d1r.at[j], d1_s.at[j], d1_rs.at[j], sib).wait_send()

        @pl.when(jnp.logical_or(zh == 1, j > 0))
        def _():
            remote(d2s.at[j], d2r.at[j], d2_s.at[j], d2_rs.at[j], far).wait_send()


        @pl.when(jnp.logical_not(jnp.logical_and(j == i0, core == half)))
        def _():
            remote(ats.at[j], atr.at[0, 0], at_s.at[j], at_rs.at[0, 0], sib).wait_send()

    loop(0, N, drain_all)

    def drain_w(h):
        head = 2 * h + core
        remote(dws.at[h, :, 1 - core], dwr.at[i0], dw_s.at[h, 1 - core], dw_rs.at[i0], sib).wait_send()

        @pl.when(head != i0)
        def _():
            remote(dws.at[h, :, core], dwr.at[i0], dw_s.at[h, core], dw_rs.at[i0], peer(head)).wait_send()

    loop(0, 8, drain_w)

    def drain_z(d):
        t = lax.rem(z + d, 8)
        remote(zs.at[lax.div(t, 4)], zr.at[z], z_s.at[t], z_rs.at[z], zpeer(t)).wait_send()

    loop(1, 8, drain_z)
    for device, rr in others:
        remote(sumkv.at[r], sumkv.at[r], sm_s.at[rr], sm_r.at[r], device).wait_send()
        remote(accsum.at[pl.ds(16 * rr, 16)], sgr.at[r], sg_s.at[rr], sg_rs.at[r], device).wait_send()


def on_device(queries, keys, values, d_out, out_weight, bar_lengths, summary_pos):
    vm = pltpu.VMEM
    dma = pltpu.SemaphoreType.DMA
    blocks = lambda n, kind=BF: vm((n, BAR, BAR), kind)
    flat = vm((BAR, WIDTH), BF)
    scratch = [
        flat, flat, flat, blocks(N), blocks(PAD + N), blocks(1 + N), blocks(1 + N),
        blocks(PAD + N), blocks(1 + N), blocks(1 + N),
        blocks(N), blocks(N),
        vm((N, 2, 2, 16, WIDTH), BF), vm((2, BAR, WIDTH), BF),
        vm((16, BAR), F32), vm((4, 16, BAR), BF), vm((BAR, BAR), BF),
        vm((256, BAR), BF), vm((NKEYS, 256), F32), vm((NKEYS, 256), BF),
        vm((NKEYS, BAR), BF), vm((BAR, NKEYS), BF),
        blocks(PAD + N, F32), vm((64, BAR), F32),
        blocks(N), blocks(N), blocks(N), blocks(N), blocks(4, F32), vm((4, 16, BAR), F32),
        blocks(N), blocks(N),
        vm((N, HEAD, BAR), BF), vm((N, HEAD, BAR), BF),
        vm((N, HEAD, BAR), BF), vm((2, 8, HEAD, BAR), BF),
        vm((8, 2, 2, 16, WIDTH), BF), vm((N, 2, 16, WIDTH), BF),
        vm((2, 16, WIDTH), F32), vm((2, 16, WIDTH), BF), vm((8, 16, WIDTH), BF),
    ]
    sems = [(5,)] + [(N,)] * 6 + [(1,)] * 2 + [(N,)] * 4 + [(1,)] * 2 + [(N,)] * 2 + [(4,)] * 2
    sems += [(N,)] * 4 + [(4,)] * 2 + [(N,)] * 4 + [(N,), (2, 8), (8, 2), (N,), (8,), (8,)]
    scratch += [dma(shape) for shape in sems]
    in_vmem = pl.BlockSpec(memory_space=pltpu.VMEM)
    in_smem = pl.BlockSpec(memory_space=pltpu.SMEM)
    rows = jax.ShapeDtypeStruct((BAR, WIDTH), BF)
    d_q, d_k, d_v, d_w = pl.pallas_call(
        kernel,
        out_shape=(rows, rows, rows, jax.ShapeDtypeStruct((16, WIDTH), F32)),
        in_specs=[pl.BlockSpec(memory_space=pltpu.HBM)] * 5 + [in_smem] * 2,
        out_specs=(in_vmem,) * 4,
        scratch_shapes=scratch,
        compiler_params=pltpu.CompilerParams(
            collective_id=0, has_side_effects=True, vmem_limit_bytes=48 * 1024 * 1024
        ),
    )(queries[0, 0], keys[0, 0], values[0, 0], d_out[0, 0], out_weight, bar_lengths, summary_pos)
    return d_q[None, None], d_k[None, None], d_v[None, None], d_w


def solution(mesh):
    spread = P("dp", "ctx", None, None)
    return jax.shard_map(
        on_device,
        mesh=mesh,
        in_specs=(spread,) * 4 + (P("ctx", None), P("dp", None), P("dp", None)),
        out_specs=(spread,) * 3 + (P("ctx", None),),
        check_vma=False,
    )
```

time: 115 us -> 107 us (0.930)
  the two profiles are of different devices: /device:TPU:14 before, /device:TPU:2 now
where the time goes in v2:
time: 107 us; the launch traced here: 105 us
  Pallas kernels  96.5 us (90%)
  local copies, waits for them, and re-layouts  7.95 us (7%)
    pallas_call x1, Pallas kernels, on_device(): pl.pallas_call(kernel, out_shape=(rows, rows, rows, jax.ShapeDtypeStruct(...  96.5 us
    unnamed x18, local copies, waits for them, and re-layouts  7.95 us

profile of v2, /device:TPU:2, one launch (start us, length us, event | category | flops | bytes accessed | tf_op | source)
XLA Modules:
  0.0 105.1 jit_solution(2522188883288272564)
XLA Ops:
  0.6 0.0 copy-start.5
  0.6 0.0 copy-start.6
  0.7 0.6 copy-done.5
  1.3 0.0 copy-done.6
  1.3 0.0 copy-start
  1.3 0.9 copy-done
  2.3 0.0 copy-start.1
  2.3 0.9 copy-done.1
  3.2 0.0 copy-start.2
  3.2 0.9 copy-done.2
  4.2 0.0 copy-start.3
  4.2 0.9 copy-done.3
  5.1 0.0 copy-start.4
  5.1 0.8 copy-done.4
  5.9 96.5 %shard_map.102 = (bf16[128,1024]{1,0:T(8,128)(2,1)S(1)}, bf16[128,1024]{1,0:T(8,128)(2,1)S(1)}, bf16[128,1024]{1,0:T(8,128)(2,1)S(1)}, f32[16,1024]{1,0:T(8,128)S(1)}) custom-call(bf16[128,1024]{1,0:T(8,128)(2,1)S(1)} %bitcast.7, bf16[128,1024]{1,0:T(8,128)(2,1)S(1)} %bitcast.8, bf16[128,1024]{1,0:T(8,128)(2,1)S(1)} %bitcast.9, ...), custom_call_target="tpu_custom_call" | custom-call | tf_op jit(solution)/shard_map/pallas_call | solution.py:589
  102.4 0.7 copy.15
  103.1 0.7 copy.16
  103.8 0.7 copy.17
  104.5 0.6 copy.18
Async XLA Ops:
  0.6 0.7 copy-start.5
  0.6 0.7 copy-start.6
  1.3 0.9 copy-start
  2.3 0.9 copy-start.1
  3.2 0.9 copy-start.2
  4.2 0.9 copy-start.3
  5.1 0.8 copy-start.4

commit v3 on v2

--- a/solution.py
+++ b/solution.py
@@ -12,6 +12,7 @@
 PAD = 8
 NKEYS = 1280
 OWN_STEPS = (1, 2, 3, 4, 6, 8)
+BEHIND = 1
 AHEAD = 6
 LAG_J = 2
 LAG = 6
@@ -48,11 +49,11 @@
 def kernel(
     q_hbm, k_hbm, v_hbm, do_hbm, w_hbm, len_ref, spot_ref,
     dq_ref, dk_ref, dv_ref, dw_ref,
-    q_ref, k_ref, v_ref, kvs, kvo, p1, p2, kvot, p1t, p2t, qgs, qgr, w4, do2, sumf, sumkv, sumt,
-    b_ref, s_ref, x_ref, cat, catt, acc, accsum, d1s, d1r, d2s, d2r, d2f, sgr,
+    q_ref, k_ref, v_ref, kvs, kvo, p1, p2, kvot, p1t, p2t, qts, qtr, gts, gtr, w4, do2, sumf, sumkv, sumt,
+    b_ref, s_ref, x_ref, pb_ref, ps, cat, catt, acc, accsum, d1s, d1r, d2s, d2r, d2f, sgr,
     fks, fkr, dqs, dqr, ats, atr, dws, dwr, wsum, zs, zr,
     in_s, kv_s, kv_r, p1_s, p1_r, p2_s, p2_r, wa_s, wa_r, wb_s, wb_r, wc_s, wc_r, do_s, do_r,
-    qg_s, qg_r, sm_s, sm_r, d1_s, d1_rs, d2_s, d2_rs, sg_s, sg_rs, fk_s, fk_rs,
+    qt_s, qt_r, gt_s, gt_r, sm_s, sm_r, d1_s, d1_rs, d2_s, d2_rs, sg_s, sg_rs, fk_s, fk_rs,
     dq_s, dq_rs, at_s, at_rs, dw_s, dw_rs, z_s, z_rs,
 ):
     dp = lax.axis_index("dp")
@@ -113,26 +114,10 @@
     loads[2].wait()
     loads[3].wait()
     loads[4].wait()
-    pl.semaphore_wait(barrier, 39)
-
-    wa = remote(w4.at[i0, zh, core], w4.at[i0, zh, core], wa_s.at[0], wa_r.at[0], far)
-    wa.start()
-
-    def send_kv(d):
-        j = rot(d)
-        remote(kvs.at[j], kvo.at[PAD + i0], kv_s.at[j], kv_r.at[i0], peer(j)).start()
-
-    loop(1, N, send_kv)
-    do_copy = remote(do2.at[core], do2.at[core], do_s.at[0], do_r.at[0], sib)
-    do_copy.start()
-    remote(w4.at[i0, 1 - zh, core], w4.at[i0, 1 - zh, core], wa_s.at[0], wa_r.at[0], far).wait_recv()
-
-    def send_w(d):
-        j = rot(d)
-        remote(w4.at[i0, :, core], w4.at[i0, :, core], wb_s.at[j], wb_r.at[i0], peer(j)).start()
-
-    loop(1, N, send_w)
-
+    for p in range(N // 2):
+        qq = (q_ref[:, 128 * p : 128 * p + 128].astype(F32) * 0.125).astype(BF)
+        qts[pl.ds(2 * p, 2)] = qq.T.reshape(2, HEAD, BAR)
+    qtr[i0] = qts[i0]
     zero = jnp.zeros((BAR, BAR), BF)
     for n in range(PAD):
         kvo[n] = zero
@@ -146,6 +131,41 @@
     acc[...] = jnp.zeros(acc.shape, F32)
     accsum[...] = jnp.zeros(accsum.shape, F32)
     wsum[...] = jnp.zeros(wsum.shape, F32)
+    pb_ref[pl.ds(0, 128), :] = zero
+    pl.semaphore_wait(barrier, 39)
+
+    wa = remote(w4.at[i0, zh, core], w4.at[i0, zh, core], wa_s.at[0], wa_r.at[0], far)
+    wa.start()
+
+    def send_kv(d):
+        j = rot(d)
+        remote(kvs.at[j], kvo.at[PAD + i0], kv_s.at[j], kv_r.at[i0], peer(j)).start()
+
+    loop(1, N, send_kv)
+
+    def send_q(d):
+        j = rot(d)
+        remote(qts.at[j], qtr.at[i0], qt_s.at[j], qt_r.at[i0], peer(j)).start()
+
+    loop(1, N, send_q)
+    do_copy = remote(do2.at[core], do2.at[core], do_s.at[0], do_r.at[0], sib)
+    do_copy.start()
+    remote(w4.at[i0, 1 - zh, core], w4.at[i0, 1 - zh, core], wa_s.at[0], wa_r.at[0], far).wait_recv()
+
+    step_u = 1 + 3 * core
+    step_v = 4 - 3 * core
+    pos_u = lax.rem(lax.div(i0, step_u), 4)
+    pos_v = lax.rem(lax.div(i0, step_v), 4)
+
+    def cell(du, dv):
+        return lax.rem(pos_u + du, 4) * step_u + lax.rem(pos_v + dv, 4) * step_v
+
+    def send_w(j, to, key):
+        at = w4.at[j, :, core]
+        remote(at, at, wb_s.at[key], wb_r.at[j], peer(to)).start()
+
+    for du in (1, 3, 2):
+        send_w(i0, cell(du, 0), cell(du, 0))
 
     row = lax.broadcasted_iota(jnp.int32, (BAR, BAR), 0)
     col = lax.broadcasted_iota(jnp.int32, (BAR, BAR), 1)
@@ -170,6 +190,13 @@
         sumf[pl.ds(j, 1), :] = jnp.sum(picked, axis=0, keepdims=True)
 
     loop(0, N, pass_on)
+    for du in (0, 1, 3, 2):
+        j = cell(du, 0)
+        if du > 0:
+            remote(w4.at[j, :, core], w4.at[j, :, core], wb_s.at[j], wb_r.at[j], peer(j)).wait_recv()
+        for dv in (1, 3, 2):
+            send_w(j, cell(0, dv), cell(du, dv))
+        remote(w4.at[j, :, core], w4.at[j, :, core], wc_s.at[j], wc_r.at[j], sib).start()
     sumkv[r] = sumf[...].astype(BF)
     r_sib = 2 * zh + (1 - core)
     r_far = 2 * (1 - zh) + core
@@ -178,37 +205,33 @@
     for device, rr in others:
         remote(sumkv.at[r], sumkv.at[r], sm_s.at[rr], sm_r.at[r], device).start()
 
-    def pass_w(d):
-        j = rot(d)
-
-        @pl.when(d > 0)
-        def _():
+    def pass_w(j, own):
+        if not own:
             remote(w4.at[j, :, core], w4.at[j, :, core], wb_s.at[j], wb_r.at[j], peer(j)).wait_recv()
-
         remote(w4.at[j, :, core], w4.at[j, :, core], wc_s.at[j], wc_r.at[j], sib).start()
 
-    loop(0, N, pass_w)
-
-    for c in range(4):
-        line = lax.rem(lax.div(i0, 4) + c, 4)
-        for n in range(4):
-            j = 4 * line + n
-            remote(w4.at[j, :, 1 - core], w4.at[j, :, 1 - core], wc_s.at[j], wc_r.at[j], sib).wait_recv()
-        rows = w4[pl.ds(4 * line, 4)].reshape(256, WIDTH)
-        g = dot_nt(do2[core], rows).astype(BF)
-        qq = q_ref[:, pl.ds(pl.multiple_of(256 * line, 256), 256)]
-        qq = (qq.astype(F32) * 0.125).astype(BF)
-        for n in range(4):
-            cols = slice(HEAD * n, HEAD * n + HEAD)
-            qgs[4 * line + n] = jnp.concatenate([qq[:, cols], g[:, cols]], axis=1)
-        for n in range(4):
-            h = 4 * line + lax.rem(i0 + n, 4)
-
-            @pl.when(i0 != h)
-            def _():
-                remote(qgs.at[h], qgr.at[i0], qg_s.at[h], qg_r.at[i0], peer(h)).start()
-
-    qgr[i0] = qgs[i0]
+    for dv in (1, 3, 2):
+        for du in (0, 1, 3, 2):
+            pass_w(cell(du, dv), False)
+
+    def project_back():
+        for c in range(4):
+            line = lax.rem(lax.div(i0, 4) + c, 4)
+            for n in range(4):
+                j = 4 * line + n
+                remote(w4.at[j, :, 1 - core], w4.at[j, :, 1 - core], wc_s.at[j], wc_r.at[j], sib).wait_recv()
+            rows = w4[pl.ds(4 * line, 4)].reshape(256, WIDTH)
+            gts[pl.ds(4 * line, 4)] = dot_nt(rows, do2[core]).astype(BF).reshape(4, HEAD, BAR)
+            for n in range(4):
+                h = 4 * line + lax.rem(i0 + n, 4)
+
+                @pl.when(i0 != h)
+                def _():
+                    remote(gts.at[h], gtr.at[i0], gt_s.at[h], gt_r.at[i0], peer(h)).start()
+
+        gtr[i0] = gts[i0]
+
+    project_back()
 
     for device, rr in others:
         remote(sumkv.at[rr], sumkv.at[rr], sm_s.at[rr], sm_r.at[rr], device).wait_recv()
@@ -307,29 +330,31 @@
 
     remote(do2.at[1 - core], do2.at[1 - core], do_s.at[0], do_r.at[0], sib).wait_recv()
 
-    def attend(i, steps):
+    def gather(i, steps, lens=None):
         bar = 4 * i + r
         blocks = [(kvo, kvot, PAD + i, 0), (p1, p1t, 1 + i - lag1, 1), (p2, p2t, 1 + i - lag2, 2)]
         blocks += [(kvo, kvot, PAD + i - m, 4 * m) for m in steps]
-        lens = []
         for n, (src, srct, at, offset) in enumerate(blocks):
             cat[pl.ds(128 * n + 128, 128), :] = src[at]
             catt[:, pl.ds(128 * n + 128, 128)] = srct[at]
-            source = bar - offset
-            length = len_ref[0, jnp.maximum(source, 0)]
-            lens.append(jnp.where(source >= 0, length, 0))
-
-        qg = qgr[i]
-        none = jnp.zeros_like(qg)
-        b_ref[pl.ds(0, 128), :] = jnp.where(left, qg, none)
-        b_ref[pl.ds(128, 128), :] = jnp.where(left, none, qg)
-        size_all = 128 * len(blocks) + 128
-        s_ref[pl.ds(0, size_all), :] = dot_nt(cat[pl.ds(0, size_all), :], b_ref[...])
-
+            if lens is not None:
+                source = bar - offset
+                length = len_ref[0, jnp.maximum(source, 0)]
+                lens.append(jnp.where(source >= 0, length, 0))
         spans = [(128 * n + 128, 128) for n in range(len(blocks))] + [(0, 64)]
+        return blocks, spans, 128 * len(blocks) + 128
+
+    nothing = jnp.zeros((HEAD, BAR), BF)
+
+    def forward(i, steps):
+        bar = 4 * i + r
+        lens = []
+        blocks, spans, size_all = gather(i, steps, lens)
+        rhs = jnp.concatenate([qtr[i], nothing], axis=0)
+        s_ref[pl.ds(0, size_all), :] = dot(cat[pl.ds(0, size_all), :], rhs)
         top = jnp.full((8, BAR), LOW, F32)
         for n, (at, size) in enumerate(spans):
-            s = s_ref[pl.ds(at, size), 0:128]
+            s = s_ref[pl.ds(at, size), :]
             if n == 0:
                 keep = (row <= col) & (row < lens[0])
             elif n < len(blocks):
@@ -337,35 +362,44 @@
             else:
                 keep = sbar < bar
             s = jnp.where(keep, s, LOW)
-            s_ref[pl.ds(at, size), 0:128] = s
+            s_ref[pl.ds(at, size), :] = s
             top = jnp.maximum(top, jnp.max(s.reshape(size // 8, 8, BAR), axis=0))
         top = jnp.max(top, axis=0, keepdims=True)
         total = jnp.zeros((8, BAR), F32)
         for at, size in spans:
-            e = jnp.exp(s_ref[pl.ds(at, size), 0:128] - top)
-            s_ref[pl.ds(at, size), 0:128] = e
+            e = jnp.exp(s_ref[pl.ds(at, size), :] - top)
+            s_ref[pl.ds(at, size), :] = e
             total = total + jnp.sum(e.reshape(size // 8, 8, BAR), axis=0)
         inv = 1.0 / jnp.sum(total, axis=0, keepdims=True)
+        for at, size in spans:
+            prob = s_ref[pl.ds(at, size), :] * inv
+            ps[i, pl.ds(at, size), :] = prob
+            pb_ref[pl.ds(at, size), :] = prob.astype(BF)
+        out = dot(catt[HEAD:BAR, pl.ds(0, size_all)], pb_ref[pl.ds(0, size_all), :])
+        ats[i] = out.astype(BF)
+
+    def backward(i, steps):
+        blocks, spans, size_all = gather(i, steps)
+        rhs = jnp.concatenate([nothing, gtr[i]], axis=0)
+        s_ref[pl.ds(0, size_all), :] = dot(cat[pl.ds(0, size_all), :], rhs)
         delta = jnp.zeros((8, BAR), F32)
         for at, size in spans:
-            prob = s_ref[pl.ds(at, size), 0:128] * inv
-            pb = prob.astype(BF)
+            pb = ps[i, pl.ds(at, size), :].astype(BF)
             x_ref[pl.ds(at, size), 128:256] = pb
-            term = pb.astype(F32) * s_ref[pl.ds(at, size), 128:256]
+            term = pb.astype(F32) * s_ref[pl.ds(at, size), :]
             delta = delta + jnp.sum(term.reshape(size // 8, 8, BAR), axis=0)
         delta = jnp.sum(delta, axis=0, keepdims=True)
         for at, size in spans:
-            prob = s_ref[pl.ds(at, size), 0:128] * inv
-            ds = prob * (s_ref[pl.ds(at, size), 128:256] - delta)
+            ds = ps[i, pl.ds(at, size), :] * (s_ref[pl.ds(at, size), :] - delta)
             x_ref[pl.ds(at, size), 0:128] = ds.astype(BF)
-
-        out = dot(catt[:, pl.ds(0, size_all)], x_ref[pl.ds(0, size_all), :])
-        dqs[i] = (out[0:HEAD, 0:128] * 0.125).astype(BF)
-        ats[i] = out[HEAD:128, 128:256].astype(BF)
-
+        qg = jnp.concatenate([qtr[i], gtr[i]], axis=0).T
+        none = jnp.zeros_like(qg)
+        b_ref[pl.ds(0, 128), :] = jnp.where(left, qg, none)
+        b_ref[pl.ds(128, 128), :] = jnp.where(left, none, qg)
         rhs = b_ref[...]
-        for n, (src, _, at, offset) in enumerate(blocks):
+        for n in (1, 2, 0) + tuple(range(3, len(blocks))):
             term = dot(x_ref[pl.ds(128 * n + 128, 128), :], rhs)
+            at = blocks[n][2]
             if n == 1:
                 d1s[i] = term.astype(BF)
                 remote(d1s.at[i], d1r.at[i], d1_s.at[i], d1_rs.at[i], sib).start()
@@ -379,8 +413,23 @@
             else:
                 acc[at] += term
         accsum[...] += dot(x_ref[pl.ds(0, 64), :], rhs)
-
-    def one_bar(t):
+        out = dot(catt[0:HEAD, pl.ds(0, size_all)], x_ref[pl.ds(0, size_all), 0:128])
+        dqs[i] = (out * 0.125).astype(BF)
+
+    def by_reach(i, work):
+        @pl.when(i >= 8)
+        def _():
+            work(i, OWN_STEPS)
+
+        @pl.when(jnp.logical_and(i >= 4, i < 8))
+        def _():
+            work(i, OWN_STEPS[:5])
+
+        @pl.when(i < 4)
+        def _():
+            work(i, OWN_STEPS[:3])
+
+    def first(t):
         i = behind(t)
 
         @pl.when(t + AHEAD < N)
@@ -393,60 +442,82 @@
 
         @pl.when(i != i0)
         def _():
-            remote(qgs.at[i], qgr.at[i], qg_s.at[i], qg_r.at[i], peer(i)).wait_recv()
-
-
-        @pl.when(i >= 8)
-        def _():
-            attend(i, OWN_STEPS)
-
-        @pl.when(jnp.logical_and(i >= 4, i < 8))
-        def _():
-            attend(i, OWN_STEPS[:5])
-
-        @pl.when(i < 4)
-        def _():
-            attend(i, OWN_STEPS[:3])
+            remote(qts.at[i], qtr.at[i], qt_s.at[i], qt_r.at[i], peer(i)).wait_recv()
+
+        by_reach(i, forward)
+        here = jnp.logical_and(i == i0, core == half)
+
+        @pl.when(jnp.logical_not(here))
+        def _():
+            remote(ats.at[i], atr.at[core, slot], at_s.at[i], at_rs.at[core, slot], near(i, half)).start()
+
+        @pl.when(here)
+        def _():
+            atr[core, slot] = ats[i]
+
+    def second(t):
+        i = behind(t)
 
         @pl.when(i != i0)
         def _():
+            remote(gts.at[i], gtr.at[i], gt_s.at[i], gt_r.at[i], peer(i)).wait_recv()
+
+        by_reach(i, backward)
+
+        @pl.when(i != i0)
+        def _():
             remote(dqs.at[i], dqr.at[i0], dq_s.at[i], dq_rs.at[i0], peer(i)).start()
 
         @pl.when(i == i0)
         def _():
             dqr[i] = dqs[i]
 
-        here = jnp.logical_and(i == i0, core == half)
-
-        @pl.when(jnp.logical_not(here))
-        def _():
-            remote(ats.at[i], atr.at[core, slot], at_s.at[i], at_rs.at[core, slot], near(i, half)).start()
-
-        @pl.when(here)
-        def _():
-            atr[core, slot] = ats[i]
-
-        @pl.when(t >= LAG_J)
-        def _():
-            join(behind(t - LAG_J))
-
-        @pl.when(t >= LAG_P)
+    def send_z(d):
+        t = lax.rem(z + d, 8)
+        remote(zs.at[lax.div(t, 4)], zr.at[z], z_s.at[t], z_rs.at[z], zpeer(t)).start()
+
+    def share_sum():
+        zs[...] = wsum[...].astype(BF)
+        loop(1, 8, send_z)
+
+    def step(t):
+        @pl.when(t < N)
+        def _():
+            first(t)
+
+        @pl.when(jnp.logical_and(t >= LAG_P, t < N + LAG_P))
         def _():
             project(t - LAG_P)
 
-        @pl.when(t >= LAG)
-        def _():
-            take_terms(t - LAG)
-
-        @pl.when(t >= LAG_W)
+        @pl.when(jnp.logical_and(t >= LAG_W, t < N + LAG_W))
         def _():
             take_dw(t - LAG_W)
 
-    loop(0, N, one_bar)
+        if LAG_W < BEHIND:
+            @pl.when(t == N + LAG_W)
+            def _():
+                share_sum()
+
+        @pl.when(t >= BEHIND)
+        def _():
+            second(t - BEHIND)
+
+        @pl.when(t >= BEHIND + LAG_J)
+        def _():
+            join(behind(t - BEHIND - LAG_J))
+
+        @pl.when(t >= BEHIND + LAG)
+        def _():
+            take_terms(t - BEHIND - LAG)
+
+    loop(0, N + BEHIND, step)
     loop(N - LAG_J, N, lambda t: join(behind(t)))
     for device, rr in others:
         remote(accsum.at[pl.ds(16 * rr, 16)], sgr.at[r], sg_s.at[rr], sg_rs.at[r], device).start()
-    loop(N - LAG_P, N, project)
+    loop(min(N, N + BEHIND - LAG_P), N, project)
+    if LAG_W >= BEHIND:
+        loop(N + BEHIND - LAG_W, N, take_dw)
+        share_sum()
     loop(N - LAG, N, take_terms)
 
     for device, rr in others:
@@ -466,15 +537,6 @@
 
     loop(0, N, finish)
     fkr[i0] = fks[i0]
-
-    loop(N - LAG_W, N, take_dw)
-    zs[...] = wsum[...].astype(BF)
-
-    def send_z(d):
-        t = lax.rem(z + d, 8)
-        remote(zs.at[lax.div(t, 4)], zr.at[z], z_s.at[t], z_rs.at[z], zpeer(t)).start()
-
-    loop(1, 8, send_z)
 
     def get_dq(d):
         j = rot(d)
@@ -516,7 +578,8 @@
         j = rot(d)
         remote(kvs.at[j], kvo.at[PAD + i0], kv_s.at[j], kv_r.at[i0], peer(j)).wait_send()
         remote(w4.at[i0, :, core], w4.at[i0, :, core], wb_s.at[j], wb_r.at[i0], peer(j)).wait_send()
-        remote(qgs.at[j], qgr.at[i0], qg_s.at[j], qg_r.at[i0], peer(j)).wait_send()
+        remote(qts.at[j], qtr.at[i0], qt_s.at[j], qt_r.at[i0], peer(j)).wait_send()
+        remote(gts.at[j], gtr.at[i0], gt_s.at[j], gt_r.at[i0], peer(j)).wait_send()
         remote(dqs.at[j], dqr.at[i0], dq_s.at[j], dq_rs.at[i0], peer(j)).wait_send()
         remote(fks.at[j], fkr.at[i0], fk_s.at[j], fk_rs.at[i0], peer(j)).wait_send()
 
@@ -567,10 +630,10 @@
     scratch = [
         flat, flat, flat, blocks(N), blocks(PAD + N), blocks(1 + N), blocks(1 + N),
         blocks(PAD + N), blocks(1 + N), blocks(1 + N),
-        blocks(N), blocks(N),
+        vm((N, HEAD, BAR), BF), vm((N, HEAD, BAR), BF), vm((N, HEAD, BAR), BF), vm((N, HEAD, BAR), BF),
         vm((N, 2, 2, 16, WIDTH), BF), vm((2, BAR, WIDTH), BF),
         vm((16, BAR), F32), vm((4, 16, BAR), BF), vm((BAR, BAR), BF),
-        vm((256, BAR), BF), vm((NKEYS, 256), F32), vm((NKEYS, 256), BF),
+        vm((256, BAR), BF), vm((NKEYS, BAR), F32), vm((NKEYS, 256), BF), vm((NKEYS, BAR), BF), vm((N, NKEYS, BAR), F32),
         vm((NKEYS, BAR), BF), vm((BAR, NKEYS), BF),
         blocks(PAD + N, F32), vm((64, BAR), F32),
         blocks(N), blocks(N), blocks(N), blocks(N), blocks(4, F32), vm((4, 16, BAR), F32),
@@ -580,7 +643,7 @@
         vm((8, 2, 2, 16, WIDTH), BF), vm((N, 2, 16, WIDTH), BF),
         vm((2, 16, WIDTH), F32), vm((2, 16, WIDTH), BF), vm((8, 16, WIDTH), BF),
     ]
-    sems = [(5,)] + [(N,)] * 6 + [(1,)] * 2 + [(N,)] * 4 + [(1,)] * 2 + [(N,)] * 2 + [(4,)] * 2
+    sems = [(5,)] + [(N,)] * 6 + [(1,)] * 2 + [(N,)] * 4 + [(1,)] * 2 + [(N,)] * 4 + [(4,)] * 2
     sems += [(N,)] * 4 + [(4,)] * 2 + [(N,)] * 4 + [(N,), (2, 8), (8, 2), (N,), (8,), (8,)]
     scratch += [dma(shape) for shape in sems]
     in_vmem = pl.BlockSpec(memory_space=pltpu.VMEM)

time: 107 us -> 106 us (level)
  no operation moved by 1% of the time
where the time goes in v3:
time: 106 us; the launch traced here: 104 us
  Pallas kernels  95.9 us (90%)
  local copies, waits for them, and re-layouts  7.95 us (8%)
    pallas_call x1, Pallas kernels, on_device(): pl.pallas_call(kernel, out_shape=(rows, rows, rows, jax.ShapeDtypeStruct(...  95.9 us
    unnamed x18, local copies, waits for them, and re-layouts  7.95 us

profile of v3, /device:TPU:2, one launch (start us, length us, event | category | flops | bytes accessed | tf_op | source)
XLA Modules:
  0.0 104.5 jit_solution(7470380872139355008)
XLA Ops:
  0.6 0.0 copy-start.5
  0.6 0.0 copy-start.6
  0.7 0.6 copy-done.5
  1.3 0.0 copy-done.6
  1.3 0.0 copy-start
  1.3 0.9 copy-done
  2.3 0.0 copy-start.1
  2.3 0.9 copy-done.1
  3.2 0.0 copy-start.2
  3.2 0.9 copy-done.2
  4.2 0.0 copy-start.3
  4.2 0.9 copy-done.3
  5.1 0.0 copy-start.4
  5.1 0.8 copy-done.4
  5.9 95.9 %shard_map.102 = (bf16[128,1024]{1,0:T(8,128)(2,1)S(1)}, bf16[128,1024]{1,0:T(8,128)(2,1)S(1)}, bf16[128,1024]{1,0:T(8,128)(2,1)S(1)}, f32[16,1024]{1,0:T(8,128)S(1)}) custom-call(bf16[128,1024]{1,0:T(8,128)(2,1)S(1)} %bitcast.7, bf16[128,1024]{1,0:T(8,128)(2,1)S(1)} %bitcast.8, bf16[128,1024]{1,0:T(8,128)(2,1)S(1)} %bitcast.9, ...), custom_call_target="tpu_custom_call" | custom-call | tf_op jit(solution)/shard_map/pallas_call | solution.py:652
  101.7 0.7 copy.15
  102.4 0.7 copy.16
  103.1 0.7 copy.17
  103.8 0.6 copy.18
Async XLA Ops:
  0.6 0.7 copy-start.5
  0.6 0.7 copy-start.6
  1.3 0.9 copy-start
  2.3 0.9 copy-start.1
  3.2 0.9 copy-start.2
  4.2 0.9 copy-start.3
  5.1 0.8 copy-start.4

commit v4 on v3

--- a/solution.py
+++ b/solution.py
@@ -13,7 +13,7 @@
 NKEYS = 1280
 OWN_STEPS = (1, 2, 3, 4, 6, 8)
 BEHIND = 1
-AHEAD = 6
+AHEAD = 4
 LAG_J = 2
 LAG = 6
 LAG_P = 4

time: 106 us -> 105 us (level)
  no operation moved by 1% of the time
where the time goes in v4:
time: 105 us; the launch traced here: 104 us
  Pallas kernels  95.3 us (91%)
  local copies, waits for them, and re-layouts  7.95 us (8%)
    pallas_call x1, Pallas kernels, on_device(): pl.pallas_call(kernel, out_shape=(rows, rows, rows, jax.ShapeDtypeStruct(...  95.3 us
    unnamed x18, local copies, waits for them, and re-layouts  7.95 us

profile of v4, /device:TPU:2, one launch (start us, length us, event | category | flops | bytes accessed | tf_op | source)
XLA Modules:
  0.0 103.9 jit_solution(10941194194521734501)
XLA Ops:
  0.6 0.0 copy-start.5
  0.6 0.0 copy-start.6
  0.7 0.6 copy-done.5
  1.3 0.0 copy-done.6
  1.3 0.0 copy-start
  1.3 0.9 copy-done
  2.3 0.0 copy-start.1
  2.3 0.9 copy-done.1
  3.2 0.0 copy-start.2
  3.2 0.9 copy-done.2
  4.2 0.0 copy-start.3
  4.2 0.9 copy-done.3
  5.1 0.0 copy-start.4
  5.1 0.8 copy-done.4
  5.9 95.3 %shard_map.102 = (bf16[128,1024]{1,0:T(8,128)(2,1)S(1)}, bf16[128,1024]{1,0:T(8,128)(2,1)S(1)}, bf16[128,1024]{1,0:T(8,128)(2,1)S(1)}, f32[16,1024]{1,0:T(8,128)S(1)}) custom-call(bf16[128,1024]{1,0:T(8,128)(2,1)S(1)} %bitcast.7, bf16[128,1024]{1,0:T(8,128)(2,1)S(1)} %bitcast.8, bf16[128,1024]{1,0:T(8,128)(2,1)S(1)} %bitcast.9, ...), custom_call_target="tpu_custom_call" | custom-call | tf_op jit(solution)/shard_map/pallas_call | solution.py:652
  101.2 0.7 copy.15
  101.9 0.7 copy.16
  102.6 0.7 copy.17
  103.3 0.6 copy.18
Async XLA Ops:
  0.6 0.7 copy-start.5
  0.6 0.7 copy-start.6
  1.3 0.9 copy-start
  2.3 0.9 copy-start.1
  3.2 0.9 copy-start.2
  4.2 0.9 copy-start.3
  5.1 0.8 copy-start.4
